TPU v7x, 128 devices: a whole 4x4x4 slice. The times are simulated.
128 devices in a mesh: dp: 8 (over z_hi, y), grp: 16 (over x, z_lo, core).
Axes of the slice: x: 4, y: 4, z: 4 (z_hi: 2, z_lo: 2; z = z_hi * 2 + z_lo), core: 2. Of those that a mesh axis runs over, the one named last changes fastest.
Arguments:
- query_latent: bfloat16 [4, 64, 1536], P(None, 'dp'), may hold values from -6 to 6
- q_up: bfloat16 [1536, 24576], P(('dp', 'grp')), may hold values from -0.15625 to 0.15625
- kv_up: bfloat16 [512, 32768], P(('dp', 'grp')), may hold values from -0.25 to 0.25
- latent_cache: bfloat16 [64, 8192, 576], P('dp', 'grp')
- new_latent: bfloat16 [4, 64, 576], P(None, 'dp'), may hold values from -6 to 6
- lengths: int32 [64], P('dp'), may hold values from 1 to 8192, as said below
Outputs:
- attn_out: bfloat16 [4, 64, 16384], P(None, 'dp', 'grp')
Inputs may be any that keep to these rules, and one draw needn't show every extreme that they name: The cache positions 0 to lengths - 1 of a request are live; some request has all 8192 positions live.
All inputs are finite; a program needn't handle non-finite values.
Results may differ from a plain program's by a relative error of at most 0.02.
Values may be sent and summed in bfloat16 or wider, within the bound.
A program may use at most 128 MiB of HBM per device.

v0:
```python
import jax
import jax.numpy as jnp
from jax import lax
from jax.sharding import PartitionSpec as P

H = 128
QL = 1536
KVL = 512
NOPE = 128
ROPE = 64
VDIM = 128
STEPS = 4


def rotate(pairs_in, position):
    half = pairs_in.shape[-1] // 2
    pairs = pairs_in.reshape(pairs_in.shape[:-1] + (half, 2))
    freq = 10000.0 ** (-(2.0 * jnp.arange(half, dtype=jnp.float32)) / pairs_in.shape[-1])
    angle = position[..., None] * freq
    first = pairs[..., 0]
    second = pairs[..., 1]
    rotated = jnp.stack(
        [
            first * jnp.cos(angle) - second * jnp.sin(angle),
            first * jnp.sin(angle) + second * jnp.cos(angle),
        ],
        -1,
    )
    return rotated.reshape(pairs_in.shape)


def cache_scores(gathered, latent_cache, lengths, first_pos, new_peak, start, heads):
    scale = float(NOPE + ROPE) ** (-0.5)
    score = (
        jnp.einsum("srhc,rkc->srhk", gathered, latent_cache, preferred_element_type=jnp.float32)
        * scale
    )
    position = first_pos + lax.broadcasted_iota(jnp.int32, (1, latent_cache.shape[1]), 1)
    live = position < lengths[:, None]
    score = jnp.where(live[None, :, None, :], score, -1e30)
    local_peak = jnp.max(score, -1)
    own = lax.dynamic_slice_in_dim(local_peak, start, heads, 2)
    local_peak = lax.dynamic_update_slice_in_dim(local_peak, jnp.maximum(own, new_peak), start, 2)
    return (score, live, local_peak)


def cache_terms(score, live, peak, latent_cache):
    prob = jnp.where(live[None, :, None, :], jnp.exp(score - peak[..., None]), 0.0)
    denom = jnp.sum(prob, -1)
    numer = jnp.einsum(
        "srhk,rkc->srhc",
        prob.astype(jnp.bfloat16),
        latent_cache[:, :, :KVL],
        preferred_element_type=jnp.float32,
    )
    return (numer, denom)


def finish(numer, denom, own_peak, new_score, new_live, new_latent, w_value, heads):
    prob = jnp.where(new_live, jnp.exp(new_score - own_peak[..., None]), 0.0)
    denom = denom + jnp.sum(prob, -1)
    numer = numer + jnp.einsum(
        "srht,trc->srhc",
        prob.astype(jnp.bfloat16),
        new_latent[:, :, :KVL],
        preferred_element_type=jnp.float32,
    )
    latent_out = (numer / denom[..., None]).astype(jnp.bfloat16)
    result = jnp.einsum("srhc,chv->srhv", latent_out, w_value, preferred_element_type=jnp.float32)
    return result.astype(jnp.bfloat16).reshape(result.shape[0], result.shape[1], heads * VDIM)


def attend(
    gathered,
    latent_cache,
    lengths,
    first_pos,
    new_peak,
    new_score,
    new_live,
    new_latent,
    w_value,
    start,
    heads,
):
    score, live, local_peak = cache_scores(
        gathered, latent_cache, lengths, first_pos, new_peak, start, heads
    )
    peak = lax.pmax(local_peak, "grp")
    numer, denom = cache_terms(score, live, peak, latent_cache)
    numer, denom = (
        lax.psum_scatter(numer.astype(jnp.bfloat16), "grp", scatter_dimension=2, tiled=True).astype(
            jnp.float32
        ),
        lax.psum_scatter(denom.astype(jnp.bfloat16), "grp", scatter_dimension=2, tiled=True).astype(
            jnp.float32
        ),
    )
    own_peak = lax.dynamic_slice_in_dim(peak, start, heads, 2)
    return finish(numer, denom, own_peak, new_score, new_live, new_latent, w_value, heads)


def per_device(query_latent, q_up, kv_up, latent_cache, new_latent, lengths):
    groups = lax.axis_size("grp")
    replicas = lax.axis_size("dp")
    heads = H // groups
    start = lax.axis_index("grp") * heads
    q_rows, kv_rows = (
        lax.all_gather(q_up, "dp", axis=0, tiled=True),
        lax.all_gather(kv_up, "dp", axis=0, tiled=True),
    )
    q_mixed, kv_mixed = (
        lax.all_to_all(q_rows, "grp", split_axis=1, concat_axis=0, tiled=True),
        lax.all_to_all(kv_rows, "grp", split_axis=1, concat_axis=0, tiled=True),
    )
    q_owned = (
        q_mixed.reshape(groups, replicas, q_up.shape[0], q_mixed.shape[1])
        .transpose(1, 0, 2, 3)
        .reshape(QL, q_mixed.shape[1])
    )
    kv_owned = (
        kv_mixed.reshape(groups, replicas, kv_up.shape[0], kv_mixed.shape[1])
        .transpose(1, 0, 2, 3)
        .reshape(KVL, kv_mixed.shape[1])
    )
    requests = query_latent.shape[1]
    q = jnp.dot(
        query_latent.reshape(STEPS * requests, QL), q_owned, preferred_element_type=jnp.float32
    )
    q = q.astype(jnp.bfloat16).reshape(STEPS, requests, heads, NOPE + ROPE)
    blocks = kv_owned.reshape(KVL, heads, NOPE + VDIM)
    w_key = blocks[:, :, :NOPE]
    w_value = blocks[:, :, NOPE:]
    q_abs = jnp.einsum("srhd,chd->srhc", q[..., :NOPE], w_key, preferred_element_type=jnp.float32)
    step_ids = lax.broadcasted_iota(jnp.int32, (STEPS, 1), 0)
    position = (lengths[None, :] + step_ids).astype(jnp.float32)
    q_rot = rotate(q[..., NOPE:].astype(jnp.float32), position[:, :, None])
    q_cat = jnp.concatenate([q_abs, q_rot], -1).astype(jnp.bfloat16)
    scale = float(NOPE + ROPE) ** (-0.5)
    new_score = (
        jnp.einsum("srhc,trc->srht", q_cat, new_latent, preferred_element_type=jnp.float32) * scale
    )
    new_live = (
        lax.broadcasted_iota(jnp.int32, (STEPS, STEPS), 1)
        <= lax.broadcasted_iota(jnp.int32, (STEPS, STEPS), 0)
    )[:, None, None, :]
    new_score = jnp.where(new_live, new_score, -1e30)
    new_peak = jnp.max(new_score, -1)
    first_pos = lax.axis_index("grp") * latent_cache.shape[1]
    results = []
    for step in range(STEPS):
        gathered = lax.all_gather(q_cat[step : step + 1], "grp", axis=2, tiled=True)
        results.append(
            attend(
                gathered,
                latent_cache,
                lengths,
                first_pos,
                new_peak[step : step + 1],
                new_score[step : step + 1],
                new_live[step : step + 1],
                new_latent,
                w_value,
                start,
                heads,
            )
        )
    return jnp.concatenate(results, 0)


def solution(mesh):
    return jax.shard_map(
        per_device,
        mesh=mesh,
        in_specs=(
            P(None, "dp", None),
            P(("dp", "grp"), None),
            P(("dp", "grp"), None),
            P("dp", "grp", None),
            P(None, "dp", None),
            P("dp"),
        ),
        out_specs=P(None, "dp", "grp"),
        check_vma=False,
    )
```

profile of v0, /device:TPU:0, one launch (start us, length us, event | category | flops | bytes accessed | tf_op | source)
XLA Modules:
  0.0 688.6 jit_solution(14816231056245481908)
XLA Ops:
  8.0 59.2 %all-gather.19.cloned.1.call-done = bf16[8,4,32768]{2,1,0:T(4,128)(2,1)} async-done(((bf16[1,4,32768]{2,1,0:T(4,128)(2,1)}), bf16[8,4,32768]{2,1,0:T(4,128)(2,1)}) %all-gather.19.cloned.1.call-update) | async-done | bytes 2097168 | tf_op jit(solution)/shard_map/all_gather | solution.py:110
  67.2 3.3 all_to_all.27
  73.0 4.4 all-to-all-start.1
  77.5 101.9 %all-gather.17.cloned.1.call-done = bf16[8,12,24576]{2,1,0:T(8,128)(2,1)} async-done(((bf16[1,12,24576]{2,1,0:T(8,128)(2,1)}), bf16[8,12,24576]{2,1,0:T(8,128)(2,1)}) %all-gather.17.cloned.1.call-update) | async-done | bytes 4718608 | tf_op jit(solution)/shard_map/all_gather | solution.py:109
  179.4 8.7 %all_to_all.24 = bf16[96,16,1536]{2,1,0:T(8,128)(2,1)} reshape(bf16[8,12,24576]{2,1,0:T(8,128)(2,1)} %all-gather.17.cloned.1.call-done) | data formatting | bytes 9437184 | tf_op jit(solution)/shard_map/all_to_all | solution.py:113
  188.2 7.1 %copy.157 = bf16[96,16,1536]{2,0,1:T(8,128)(2,1)} copy(bf16[96,16,1536]{2,1,0:T(8,128)(2,1)} %all_to_all.24) | data formatting | bytes 9437184 | tf_op jit(solution)/shard_map/all_to_all | solution.py:113
  195.2 4.7 all-to-all-start
  201.7 2.9 copy.163
  204.6 3.2 reshape_reshape.3
  209.0 51.2 %all-to-all-done = bf16[96,16,1536]{2,0,1:T(8,128)(2,1)} async-done(((bf16[96,16,1536]{2,0,1:T(8,128)(2,1)}), bf16[96,16,1536]{2,0,1:T(8,128)(2,1)}, u32[]{:S(2)}, u32[]{:S(2)}) %all-to-all-start) | async-done | bytes 4718624 | tf_op jit(solution)/shard_map/all_to_all | solution.py:113
  260.2 4.9 copy.158
  265.1 5.7 copy.159
  270.7 8.2 %reshape.307 = bf16[1536,1536]{1,0:T(8,128)(2,1)} reshape(bf16[8,16,12,1536]{3,2,1,0:T(8,128)(2,1)} %copy.159) | data formatting | bytes 9437184 | tf_op jit(solution)/shard_map/reshape | solution.py:119
  279.0 3.2 convolution_convert_fusion
  288.3 35.9 %all-gather.11.cloned.1.call-done = bf16[1,8,128,576]{3,1,0,2:T(8,128)(2,1)} async-done(((bf16[1,8,8,576]{3,1,0,2:T(8,128)(2,1)}), bf16[1,8,128,576]{3,1,0,2:T(8,128)(2,1)}) %all-gather.11.cloned.1.call-update) | async-done | bytes 1179664 | tf_op jit(solution)/shard_map/all_gather | solution.py:152
  326.4 32.3 %all-gather.9.cloned.1.call-done = bf16[1,8,128,576]{3,1,0,2:T(8,128)(2,1)} async-done(((bf16[1,8,8,576]{3,1,0,2:T(8,128)(2,1)}), bf16[1,8,128,576]{3,1,0,2:T(8,128)(2,1)}) %all-gather.9.cloned.1.call-update) | async-done | bytes 1179664 | tf_op jit(solution)/shard_map/all_gather | solution.py:152
  358.7 2.8 copy.167
  361.5 3.5 fusion.52
  368.5 29.8 %all-reduce.5 = (f32[1,8,128]{2,1,0:T(8,128)S(1)}, f32[1,8,128]{2,1,0:T(8,128)S(1)}) all-reduce(f32[1,8,128]{2,1,0:T(8,128)S(1)} %dynamic_update_slice.12, f32[1,8,128]{2,1,0:T(8,128)S(1)} %dynamic_update_slice.13), channel_id=1, replica_groups=mesh['dp'=8,'grp'=16] {'grp'}, use_global_device_ids=true, to_apply=%region_2.3 | all-reduce | flops 2048 | bytes 16384 | tf_op jit(solution)/shard_map/pmax | solution.py:89
  398.3 4.4 fusion.195
  404.7 3.7 fusion.200
  411.8 16.1 %all-gather.13.cloned.1.call-done = bf16[1,8,128,576]{3,1,0,2:T(8,128)(2,1)} async-done(((bf16[1,8,8,576]{3,1,0,2:T(8,128)(2,1)}), bf16[1,8,128,576]{3,1,0,2:T(8,128)(2,1)}) %all-gather.13.cloned.1.call-update) | async-done | bytes 1179664 | tf_op jit(solution)/shard_map/all_gather | solution.py:152
  427.9 2.8 copy.178
  430.7 3.5 fusion.48
  435.3 5.5 fusion.28
  441.2 29.8 %all-reduce.4 = (f32[1,8,128]{2,1,0:T(8,128)S(1)}, f32[1,8,128]{2,1,0:T(8,128)S(1)}) all-reduce(f32[1,8,128]{2,1,0:T(8,128)S(1)} %dynamic_update_slice.15, f32[1,8,128]{2,1,0:T(8,128)S(1)} %dynamic_update_slice.14), channel_id=1, replica_groups=mesh['dp'=8,'grp'=16] {'grp'}, use_global_device_ids=true, to_apply=%region_20.21 | all-reduce | flops 2048 | bytes 16384 | tf_op jit(solution)/shard_map/pmax | solution.py:89
  471.0 4.4 fusion.205
  478.1 3.7 fusion.190
  485.3 27.7 %all-reduce.6 = (bf16[1,8,128]{2,1,0:T(8,128)(2,1)S(1)}, bf16[1,8,128]{2,1,0:T(8,128)(2,1)S(1)}, bf16[1,8,128]{2,1,0:T(8,128)(2,1)S(1)}, bf16[1,8,128]{2,1,0:T(8,128)(2,1)S(1)}) all-reduce(bf16[1,8,128]{2,1,0:T(8,128)(2,1)S(1)} %bitcast.518, bf16[1,8,128]{2,1,0:T(8,128)(2,1)S(1)} %bitcast.517, ...), channel_id=9, replica_groups=mesh['dp'=8,'grp'=16] {'grp'}, use_global_device_ids=true, to_apply=%region_23.24.clone | all-reduce | flops 4096 | bytes 16384
  514.2 40.4 %reduce-scatter.19.cloned.1.call-done = bf16[8,4096]{1,0:T(8,128)(2,1)} async-done(((bf16[128,4096]{1,0:T(8,128)(2,1)}), bf16[8,4096]{1,0:T(8,128)(2,1)}) %reduce-scatter.19.cloned.1.call-update) | async-done | bytes 65552
  555.5 61.8 %reduce-scatter.21.cloned.1.call-done = bf16[8,4096]{1,0:T(8,128)(2,1)} async-done(((bf16[128,4096]{1,0:T(8,128)(2,1)}), bf16[8,4096]{1,0:T(8,128)(2,1)}) %reduce-scatter.21.cloned.1.call-update) | async-done | bytes 65552
  619.9 59.7 %reduce-scatter.23.cloned.1.call-done = bf16[8,4096]{1,0:T(8,128)(2,1)} async-done(((bf16[128,4096]{1,0:T(8,128)(2,1)}), bf16[8,4096]{1,0:T(8,128)(2,1)}) %reduce-scatter.23.cloned.1.call-update) | async-done | bytes 65552
  (123 shorter events, 37.4 us)
Async XLA Ops:
  6.5 272.4 %copy-start = (bf16[4,8,1536]{2,1,0:T(8,128)(2,1)S(1)}, bf16[4,8,1536]{2,1,0:T(8,128)(2,1)}, u32[]{:S(2)}) copy-start(bf16[4,8,1536]{2,1,0:T(8,128)(2,1)} %param.6) | copy-start | bytes 294916
  6.5 60.7 %all-gather.19.cloned.1.call-start = ((), (), s32[]{:S(2)}) async-start(), calls=%async_computation.11 | async-start | bytes 2359296 | tf_op jit(solution)/shard_map/all_gather | solution.py:110
  7.3 172.2 %all-gather.17.cloned.1.call-start = ((), (), s32[]{:S(2)}) async-start(), calls=%async_computation.10 | async-start | bytes 7077888 | tf_op jit(solution)/shard_map/all_gather | solution.py:109
  73.0 122.2 %all-to-all-start.1 = ((bf16[32,16,2048]{2,0,1:T(8,128)(2,1)}), bf16[32,16,2048]{2,0,1:T(8,128)(2,1)S(1)}, u32[]{:S(2)}, u32[]{:S(2)}) async-start(bf16[32,16,2048]{2,0,1:T(8,128)(2,1)} %copy.161), calls=%async_computation.1 | async-start | bytes 4194304 | tf_op jit(solution)/shard_map/all_to_all | solution.py:114
  195.2 5.0 copy-start.12
  195.2 64.9 %all-to-all-start = ((bf16[96,16,1536]{2,0,1:T(8,128)(2,1)}), bf16[96,16,1536]{2,0,1:T(8,128)(2,1)}, u32[]{:S(2)}, u32[]{:S(2)}) async-start(bf16[96,16,1536]{2,0,1:T(8,128)(2,1)} %copy.157), calls=%async_computation | async-start | bytes 9437184 | tf_op jit(solution)/shard_map/all_to_all | solution.py:113
  199.9 124.3 %all-gather.11.cloned.1.call-start = ((), (), s32[]{:S(2)}) async-start(), calls=%async_computation.7 | async-start | bytes 1392640 | tf_op jit(solution)/shard_map/all_gather | solution.py:152
  282.7 1.2 copy-start.8
  283.2 4.1 copy-start.11
  285.2 73.5 %all-gather.9.cloned.1.call-start = ((), (), s32[]{:S(2)}) async-start(), calls=%async_computation.6 | async-start | bytes 1392640 | tf_op jit(solution)/shard_map/all_gather | solution.py:152
  285.8 123.8 %all-gather.15.cloned.1.call-start = ((), (), s32[]{:S(2)}) async-start(), calls=%async_computation.9 | async-start | bytes 1392640 | tf_op jit(solution)/shard_map/all_gather | solution.py:152
  286.4 141.6 %all-gather.13.cloned.1.call-start = ((), (), s32[]{:S(2)}) async-start(), calls=%async_computation.8 | async-start | bytes 1392640 | tf_op jit(solution)/shard_map/all_gather | solution.py:152
  286.9 226.4 %reduce-scatter.17.cloned.1.call-start = ((), (), s32[]{:S(2)}) async-start(), calls=%async_computation.12 | async-start | bytes 1114112
  358.7 6.3 slice-start
  361.5 3.6 slice-start.1
  361.5 3.9 copy-start.7
  365.5 2.6 copy-start.4
  402.7 2.0 copy-start.5
  403.9 150.7 %reduce-scatter.19.cloned.1.call-start = ((), (), s32[]{:S(2)}) async-start(), calls=%async_computation.13 | async-start | bytes 1114112
  409.5 207.8 %reduce-scatter.21.cloned.1.call-start = ((), (), s32[]{:S(2)}) async-start(), calls=%async_computation.14 | async-start | bytes 1114112
  427.9 6.3 slice-start.2
  430.7 3.6 slice-start.3
  430.7 4.3 copy-start.6
  430.7 4.6 copy-start.10
  435.3 5.5 copy-start.2
  475.4 1.5 copy-start.13
  475.4 2.7 copy-start.3
  476.5 203.1 %reduce-scatter.23.cloned.1.call-start = ((), (), s32[]{:S(2)}) async-start(), calls=%async_computation.15 | async-start | bytes 1114112
  481.9 2.0 copy-start.9
  619.0 62.7 %copy-start.1 = (bf16[4,8,1536]{2,1,0:T(8,128)(2,1)S(1)}, bf16[4,8,1536]{2,1,0:T(8,128)(2,1)}, u32[]{:S(2)}) copy-start(bf16[4,8,1536]{2,1,0:T(8,128)(2,1)} %param.6) | copy-start | bytes 294916
Sparse Core Ops, SparseCore 0:
  9.7 57.4 all-gather.18
  69.5 109.8 all-gather.16
  285.3 38.8 all-gather.10
  325.8 32.9 all-gather.8
  360.3 32.9 all-gather.14
  394.9 32.9 all-gather.12
  430.3 61.7 reduce-scatter.16
  494.6 60.0 reduce-scatter.18
  557.0 60.2 reduce-scatter.20
  619.6 59.9 reduce-scatter.22
where the time goes:
time: 690 us; the launch traced here: 689 us
  waiting for transfers between devices  462 us (67%)
  blocking collectives  87.3 us (13%)
  local copies, waits for them, and re-layouts  72.2 us (10%)
  matrix products  38.4 us (6%)
  between operations  14.6 us (2%)
  starting transfers between devices  10.2 us (1%)
    unnamed x14, waiting for transfers between devices  165 us
    all_gather x1, waiting for transfers between devices, per_device(): lax.all_gather(q_up, 'dp', axis=0, tiled=True)  102 us
    all_gather x4, waiting for transfers between devices, per_device(): gathered = lax.all_gather(q_cat[step:step + 1], 'grp', axis=2, tiled=True)  84.4 us
    pmax x2, blocking collectives, attend(): peak = lax.pmax(local_peak, 'grp')  59.6 us
    all_gather x1, waiting for transfers between devices, per_device(): lax.all_gather(kv_up, 'dp', axis=0, tiled=True)  59.2 us
    all_to_all x1, waiting for transfers between devices, per_device(): lax.all_to_all(q_rows, 'grp', split_axis=1, concat_axis=0, tiled=True)  51.2 us
    unnamed x1, blocking collectives  27.7 us
    all_to_all x3, local copies, waits for them, and re-layouts, per_device(): lax.all_to_all(q_rows, 'grp', split_axis=1, concat_axis=0, tiled=True)  20.7 us
  transfers between devices with their start and end apart: 12, of which 9 were waited for; matrix products, arithmetic and copies ran while one was open for 11% of the time, Pallas kernels for 0%

commit v1 on v0

v1 whole, which is shorter than its diff:
```python
import jax
import jax.numpy as jnp
from jax import lax
from jax.experimental import pallas as pl
from jax.experimental.pallas import tpu as pltpu
from jax.sharding import PartitionSpec as P

MESH = pl.DeviceIdType.MESH

H = 128
QL = 1536
KVL = 512
NOPE = 128
ROPE = 64
VDIM = 128
STEPS = 4
WIDTH = KVL + ROPE
LOG2E = 1.4426950408889634


def rotate(pairs_in, position):
    half = pairs_in.shape[-1] // 2
    pairs = pairs_in.reshape(pairs_in.shape[:-1] + (half, 2))
    freq = 10000.0 ** (-(2.0 * jnp.arange(half, dtype=jnp.float32)) / pairs_in.shape[-1])
    angle = position[..., None] * freq
    first = pairs[..., 0]
    second = pairs[..., 1]
    rotated = jnp.stack(
        [
            first * jnp.cos(angle) - second * jnp.sin(angle),
            first * jnp.sin(angle) + second * jnp.cos(angle),
        ],
        -1,
    )
    return rotated.reshape(pairs_in.shape)


class Copies:
    def __init__(self, send_sem, recv_sem):
        self.send_sem, self.recv_sem, self.sent = send_sem, recv_sem, []

    def send(self, src, dst, peer):
        k = len(self.sent)
        copy = pltpu.make_async_remote_copy(
            src_ref=src,
            dst_ref=dst,
            send_sem=self.send_sem.at[k],
            recv_sem=self.recv_sem.at[k],
            device_id={"grp": peer},
            device_id_type=MESH,
        )
        copy.start()
        self.sent.append(copy)
        return copy

    def finish(self):
        for copy in self.sent:
            copy.wait_send()


def merge(a, b):
    peak = jnp.maximum(a[0], b[0])
    return peak, a[1] * jnp.exp2(a[0] - peak) + b[1] * jnp.exp2(b[0] - peak)


def attend_kernel(
    own_ref, cache_ref, new_ref, len_ref, wv_ref, out_ref,
    G, K, O, NB, RD, T, RF, RL, RR, RL1, RR1, RZ0, RZ1, U0, V1, M, L, ml_send, ml_recv, SC, SCT, F,
    send_sem, recv_sem, cache_sem,
):
    gi = lax.axis_index("grp")
    x, zl, c = gi // 4, (gi // 2) % 2, gi % 2
    xp, xm, x2 = (x + 1) % 4, (x + 3) % 4, (x + 2) % 4
    zo, co = 1 - zl, 1 - c

    def at(xx, zz, cc):
        return xx * 4 + zz * 2 + cc

    p_xp, p_xm, p_x2 = at(xp, zl, c), at(xm, zl, c), at(x2, zl, c)
    p_z, p_c = at(x, zo, c), at(x, zl, co)

    load = pltpu.make_async_copy(cache_ref, K, cache_sem)
    load.start()
    barrier = pltpu.get_barrier_semaphore()
    for peer in (p_xp, p_xm, p_x2, p_z, p_c):
        pl.semaphore_signal(barrier, inc=1, device_id={"grp": peer}, device_id_type=MESH)
    G[:, pl.ds(gi, 1)] = own_ref[...][:, None]
    pl.semaphore_wait(barrier, 5)

    net = Copies(send_sem, recv_sem)

    def pass_on(first, count, slot, peer):
        block = G.at[pl.ds(first, count), slot]
        return net.send(block, block, peer)

    s_l, s_r, s_z = p_xm, p_xp, p_z
    s_lz, s_rz, s_f, s_fz = at(xm, zo, c), at(xp, zo, c), p_x2, at(x2, zo, c)
    mate = []
    z0 = pass_on(0, 4, gi, p_z)
    l0 = pass_on(0, 4, gi, p_xp)
    r0 = pass_on(0, 4, gi, p_xm)
    l1 = pass_on(4, 4, gi, p_xp)
    r1 = pass_on(4, 4, gi, p_xm)
    mate.append(pass_on(0, 8, gi, p_c))
    z1 = pass_on(4, 4, gi, p_z)
    z0.wait_recv()
    lz0 = pass_on(0, 4, s_z, p_xp)
    rz0 = pass_on(0, 4, s_z, p_xm)
    mate.append(pass_on(0, 4, s_z, p_c))
    l0.wait_recv()
    fa0 = pass_on(0, 2, s_l, p_xp)
    mate.append(pass_on(0, 4, s_l, p_c))
    r0.wait_recv()
    fb0 = pass_on(2, 2, s_r, p_xm)
    mate.append(pass_on(0, 4, s_r, p_c))
    l1.wait_recv()
    fa1 = pass_on(4, 2, s_l, p_xp)
    lz1 = pass_on(4, 4, s_l, p_z)
    mate.append(pass_on(4, 4, s_l, p_c))
    r1.wait_recv()
    fb1 = pass_on(6, 2, s_r, p_xm)
    rz1 = pass_on(4, 4, s_r, p_z)
    mate.append(pass_on(4, 4, s_r, p_c))
    lz0.wait_recv()
    fza0 = pass_on(0, 2, s_lz, p_xp)
    mate.append(pass_on(0, 4, s_lz, p_c))
    rz0.wait_recv()
    fzb0 = pass_on(2, 2, s_rz, p_xm)
    mate.append(pass_on(0, 4, s_rz, p_c))
    fa0.wait_recv()
    mate.append(pass_on(0, 2, s_f, p_c))
    fb0.wait_recv()
    mate.append(pass_on(2, 2, s_f, p_c))
    fa1.wait_recv()
    fza1 = pass_on(4, 2, s_f, p_z)
    mate.append(pass_on(4, 2, s_f, p_c))
    fb1.wait_recv()
    fzb1 = pass_on(6, 2, s_f, p_z)
    mate.append(pass_on(6, 2, s_f, p_c))
    z1.wait_recv()
    mate.append(pass_on(4, 4, s_z, p_c))
    fza0.wait_recv()
    mate.append(pass_on(0, 2, s_fz, p_c))
    fzb0.wait_recv()
    mate.append(pass_on(2, 2, s_fz, p_c))
    lz1.wait_recv()
    mate.append(pass_on(4, 4, s_lz, p_c))
    rz1.wait_recv()
    mate.append(pass_on(4, 4, s_rz, p_c))
    fza1.wait_recv()
    mate.append(pass_on(4, 2, s_fz, p_c))
    fzb1.wait_recv()
    mate.append(pass_on(6, 2, s_fz, p_c))
    for copy in mate:
        copy.wait_recv()
    load.wait()

    to_log2 = float(NOPE + ROPE) ** -0.5 * LOG2E
    lane = lax.broadcasted_iota(jnp.int32, (512, 128), 1)
    key_at = lax.broadcasted_iota(jnp.int32, (1, 512), 1) + gi * 512
    new_live = lax.broadcasted_iota(jnp.int32, (32, 16), 1) <= (
        lax.broadcasted_iota(jnp.int32, (32, 16), 0) % 4
    )
    nt = (((1,), (1,)), ((), ()))
    rows = pl.ds(gi * 32, 32)

    def one_request(r, carry):
        q = G[r].reshape(512, WIDTH)
        k = K[r]
        kn = new_ref[r]
        s = lax.dot_general(q, k, nt, preferred_element_type=jnp.float32) * to_log2
        s = jnp.where(key_at < len_ref[pl.ds(r, 1), :], s, -1e30)
        sn = lax.dot_general(G[r, gi], kn, nt, preferred_element_type=jnp.float32) * to_log2
        sn = jnp.where(new_live, sn, -1e30)
        M[...] = jnp.broadcast_to(jnp.maximum(jnp.max(s, 1, keepdims=True), -1e29), (512, 128))
        M[rows, :] = jnp.maximum(M[rows, :], jnp.max(sn, 1, keepdims=True))
        p = jnp.exp2(s - M[:, 0:1])
        pn = jnp.exp2(sn - M[rows, 0:1])
        L[...] = jnp.broadcast_to(jnp.sum(p, 1, keepdims=True), (512, 128))
        L[rows, :] = L[rows, :] + jnp.sum(pn, 1, keepdims=True)
        O[r] = jnp.dot(p.astype(jnp.bfloat16), k[:, :KVL], preferred_element_type=jnp.float32)
        O[r, rows, :] = O[r, rows, :] + jnp.dot(
            pn.astype(jnp.bfloat16), kn[:, :KVL], preferred_element_type=jnp.float32
        )
        both = jnp.transpose(jnp.where(lane == 0, M[...], L[...]))
        ml_send[0, 0, pl.ds(r, 1), :] = both[0:1]
        ml_send[0, 1, pl.ds(r, 1), :] = both[1:2]
        return carry

    lax.fori_loop(0, 8, one_request, 0)

    mine = (ml_send[0, 0], ml_send[0, 1])
    total = mine
    for stage, peer in ((0, p_c), (1, p_z)):
        copy = net.send(ml_send.at[stage], ml_recv.at[stage], peer)
        copy.wait_recv()
        total = merge(total, (ml_recv[stage, 0], ml_recv[stage, 1]))
        ml_send[stage + 1, 0] = total[0]
        ml_send[stage + 1, 1] = total[1]
    last = [net.send(ml_send.at[2], ml_recv.at[2 + j], p) for j, p in enumerate((p_xp, p_xm, p_x2))]
    for j, copy in enumerate(last):
        copy.wait_recv()
        total = merge(total, (ml_recv[2 + j, 0], ml_recv[2 + j, 1]))
    SC[...] = jnp.zeros_like(SC)
    SC[0:8, :] = jnp.exp2(mine[0] - total[0]) / total[1]
    SCT[...] = jnp.transpose(SC[...])

    halves = []
    for r in range(8):
        part = (O[r] * SCT[:, r : r + 1]).astype(jnp.bfloat16)
        NB[r] = part.reshape(4, 2, 2, 32, KVL)
        if r % 4 == 3:
            span = pl.ds(r - 3, 4)
            halves.append(net.send(NB.at[span, :, :, co], RD.at[span], p_c))

    def add(a, b):
        return (a.astype(jnp.float32) + b.astype(jnp.float32)).astype(jnp.bfloat16)

    for h in range(2):
        halves[h].wait_recv()
        for r in range(4 * h, 4 * h + 4):
            T[r] = add(NB[r, :, :, c], RD[r])
        if h == 0:
            fa = net.send(T.at[0:2, x2], RF.at[0], p_xp)
            fb = net.send(T.at[2:4, x2], RF.at[1], p_xm)
    zr = net.send(T.at[4:8, :, zo], RZ1, p_z)
    fa.wait_recv()
    T[0:2, xp] = add(T[0:2, xp], RF[0])
    to_r = net.send(T.at[0:4, xp], RL, p_xp)
    fb.wait_recv()
    T[2:4, xm] = add(T[2:4, xm], RF[1])
    to_l = net.send(T.at[0:4, xm], RR, p_xm)
    zr.wait_recv()
    for r in range(4):
        V1[r] = add(T[4 + r, :, zl], RZ1[r])
    ga = net.send(V1.at[0:2, x2], RF.at[2, :, 0], p_xp)
    gb = net.send(V1.at[2:4, x2], RF.at[2, :, 1], p_xm)
    to_r.wait_recv()
    to_l.wait_recv()
    U0[...] = (
        T[0:4, x].astype(jnp.float32) + RL[...].astype(jnp.float32) + RR[...].astype(jnp.float32)
    ).astype(jnp.bfloat16)
    zz = net.send(U0.at[:, zo], RZ0, p_z)
    ga.wait_recv()
    V1[0:2, xp] = add(V1[0:2, xp], RF[2, :, 0])
    to_r1 = net.send(V1.at[:, xp], RL1, p_xp)
    gb.wait_recv()
    V1[2:4, xm] = add(V1[2:4, xm], RF[2, :, 1])
    to_l1 = net.send(V1.at[:, xm], RR1, p_xm)
    zz.wait_recv()
    F[0:4] = add(U0[:, zl], RZ0[...])
    to_r1.wait_recv()
    to_l1.wait_recv()
    F[4:8] = (
        V1[:, x].astype(jnp.float32) + RL1[...].astype(jnp.float32) + RR1[...].astype(jnp.float32)
    ).astype(jnp.bfloat16)

    to = lax.broadcasted_iota(jnp.int32, (256, 256), 0)
    was = lax.broadcasted_iota(jnp.int32, (256, 256), 1)
    move = (was == (to % 8) * 32 + to // 8).astype(jnp.bfloat16)
    latent = jnp.dot(
        move, F[...].reshape(256, KVL), preferred_element_type=jnp.float32
    ).astype(jnp.bfloat16)
    for i in range(8):
        out_ref[:, i * VDIM : (i + 1) * VDIM] = jnp.dot(
            latent[i * 32 : (i + 1) * 32], wv_ref[i], preferred_element_type=jnp.float32
        ).astype(jnp.bfloat16)
    net.finish()


def attend(own, cache, new_latent, lengths, w_value):
    fresh = jnp.pad(new_latent.transpose(1, 0, 2), ((0, 0), (0, 16 - STEPS), (0, 0)))
    limit = jnp.broadcast_to(lengths[:, None], (8, 512))
    vmem = pl.BlockSpec(memory_space=pltpu.VMEM)
    bf, f32 = jnp.bfloat16, jnp.float32
    copies = 64
    return pl.pallas_call(
        attend_kernel,
        out_shape=jax.ShapeDtypeStruct((32, 8 * VDIM), bf),
        in_specs=[vmem, pl.BlockSpec(memory_space=pl.ANY), vmem, vmem, vmem],
        out_specs=vmem,
        scratch_shapes=[
            pltpu.VMEM((8, 16, 32, WIDTH), bf),
            pltpu.VMEM((8, 512, WIDTH), bf),
            pltpu.VMEM((8, 512, KVL), f32),
            pltpu.VMEM((8, 4, 2, 2, 32, KVL), bf),
            pltpu.VMEM((8, 4, 2, 32, KVL), bf),
            pltpu.VMEM((8, 4, 2, 32, KVL), bf),
            pltpu.VMEM((3, 2, 2, 32, KVL), bf),
            pltpu.VMEM((4, 2, 32, KVL), bf),
            pltpu.VMEM((4, 2, 32, KVL), bf),
            pltpu.VMEM((4, 32, KVL), bf),
            pltpu.VMEM((4, 32, KVL), bf),
            pltpu.VMEM((4, 32, KVL), bf),
            pltpu.VMEM((4, 4, 32, KVL), bf),
            pltpu.VMEM((4, 2, 32, KVL), bf),
            pltpu.VMEM((4, 4, 32, KVL), bf),
            pltpu.VMEM((512, 128), f32),
            pltpu.VMEM((512, 128), f32),
            pltpu.VMEM((3, 2, 8, 512), f32),
            pltpu.VMEM((5, 2, 8, 512), f32),
            pltpu.VMEM((128, 512), f32),
            pltpu.VMEM((512, 128), f32),
            pltpu.VMEM((8, 32, KVL), bf),
            pltpu.SemaphoreType.DMA((copies,)),
            pltpu.SemaphoreType.DMA((copies,)),
            pltpu.SemaphoreType.DMA,
        ],
        compiler_params=pltpu.CompilerParams(
            collective_id=1, has_side_effects=True, vmem_limit_bytes=56 * 1024 * 1024
        ),
    )(own, cache, fresh, limit, w_value)


def per_device(query_latent, q_up, kv_up, latent_cache, new_latent, lengths):
    groups = lax.axis_size("grp")
    replicas = lax.axis_size("dp")
    heads = H // groups
    q_rows, kv_rows = (
        lax.all_gather(q_up, "dp", axis=0, tiled=True),
        lax.all_gather(kv_up, "dp", axis=0, tiled=True),
    )
    q_mixed, kv_mixed = (
        lax.all_to_all(q_rows, "grp", split_axis=1, concat_axis=0, tiled=True),
        lax.all_to_all(kv_rows, "grp", split_axis=1, concat_axis=0, tiled=True),
    )
    q_owned = (
        q_mixed.reshape(groups, replicas, q_up.shape[0], q_mixed.shape[1])
        .transpose(1, 0, 2, 3)
        .reshape(QL, q_mixed.shape[1])
    )
    kv_owned = (
        kv_mixed.reshape(groups, replicas, kv_up.shape[0], kv_mixed.shape[1])
        .transpose(1, 0, 2, 3)
        .reshape(KVL, kv_mixed.shape[1])
    )
    requests = query_latent.shape[1]
    q = jnp.dot(
        query_latent.reshape(STEPS * requests, QL), q_owned, preferred_element_type=jnp.float32
    )
    q = q.astype(jnp.bfloat16).reshape(STEPS, requests, heads, NOPE + ROPE)
    blocks = kv_owned.reshape(KVL, heads, NOPE + VDIM)
    w_key = blocks[:, :, :NOPE]
    w_value = blocks[:, :, NOPE:]
    q_abs = jnp.einsum("srhd,chd->srhc", q[..., :NOPE], w_key, preferred_element_type=jnp.float32)
    step_ids = lax.broadcasted_iota(jnp.int32, (STEPS, 1), 0)
    position = (lengths[None, :] + step_ids).astype(jnp.float32)
    q_rot = rotate(q[..., NOPE:].astype(jnp.float32), position[:, :, None])
    q_cat = jnp.concatenate([q_abs, q_rot], -1).astype(jnp.bfloat16)
    own = q_cat.transpose(1, 2, 0, 3).reshape(requests, heads * STEPS, WIDTH)
    out = attend(own, latent_cache, new_latent, lengths, w_value.transpose(1, 0, 2))
    return out.reshape(STEPS, requests, heads * VDIM)


def solution(mesh):
    return jax.shard_map(
        per_device,
        mesh=mesh,
        in_specs=(
            P(None, "dp", None),
            P(("dp", "grp"), None),
            P(("dp", "grp"), None),
            P("dp", "grp", None),
            P(None, "dp", None),
            P("dp"),
        ),
        out_specs=P(None, "dp", "grp"),
        check_vma=False,
    )
```

time: 690 us -> 371 us (0.54)
  waiting for transfers between devices: 462 us -> 205 us
  blocking collectives: 87.3 us -> 0 us
  Pallas kernels: 0 us -> 75.2 us
  matrix products: 38.4 us -> 3.69 us
  local copies, waits for them, and re-layouts: 72.2 us -> 61.2 us
    unnamed x14 -> x2, waiting for transfers between devices: 165 us -> 1.41 us
    all_gather x4 -> x0, waiting for transfers between devices: 84.4 us -> none  [per_device(): gathered = lax.all_gather(q_cat[step:step + 1], 'grp', axis=2, tiled=True)]
    pallas_call x0 -> x1, Pallas kernels: none -> 75.2 us  [attend(): pl.pallas_call(attend_kernel, out_shape=jax.ShapeDtypeStruct((32, 8 * VDI...]
    pmax x2 -> x0, blocking collectives: 59.6 us -> none  [attend(): peak = lax.pmax(local_peak, 'grp')]
    dot_general x17 -> x0, matrix products: 34.7 us -> none  [the longest x4 16.2 us: cache_terms(): jnp.einsum('srhk,rkc->srhc', prob.astype(jnp.bfloat16), latent_cache[:, :...]
    unnamed x1 -> x0, blocking collectives: 27.7 us -> none
    all_gather x4 -> x0, local copies, waits for them, and re-layouts: 9.98 us -> none  [per_device(): gathered = lax.all_gather(q_cat[step:step + 1], 'grp', axis=2, tiled=True)]
    all_to_all x1, waiting for transfers between devices: 51.2 us -> 42.3 us  [per_device(): lax.all_to_all(q_rows, 'grp', split_axis=1, concat_axis=0, tiled=True)]
  transfers between devices with their start and end apart: 12 -> 4, of which waited for: 9 -> 3; matrix products, arithmetic and copies ran while one was open for 11% -> 7% of each run, Pallas kernels for 0% -> 0%
where the time goes in v1:
time: 371 us; the launch traced here: 369 us
  waiting for transfers between devices  205 us (55%)
  Pallas kernels  75.2 us (20%)
  local copies, waits for them, and re-layouts  61.2 us (16%)
  between operations  13.6 us (4%)
  starting transfers between devices  9.22 us (2%)
    all_gather x1, waiting for transfers between devices, per_device(): lax.all_gather(q_up, 'dp', axis=0, tiled=True)  102 us
    pallas_call x1, Pallas kernels, attend(): pl.pallas_call(attend_kernel, out_shape=jax.ShapeDtypeStruct((32, 8 * VDI...  75.2 us
    all_gather x1, waiting for transfers between devices, per_device(): lax.all_gather(kv_up, 'dp', axis=0, tiled=True)  59.2 us
    all_to_all x1, waiting for transfers between devices, per_device(): lax.all_to_all(q_rows, 'grp', split_axis=1, concat_axis=0, tiled=True)  42.3 us
    all_to_all x3, local copies, waits for them, and re-layouts, per_device(): lax.all_to_all(q_rows, 'grp', split_axis=1, concat_axis=0, tiled=True)  20.8 us
    unnamed x11, local copies, waits for them, and re-layouts  10.7 us
    reshape x1, local copies, waits for them, and re-layouts, per_device(): q_owned = q_mixed.reshape(groups, replicas, q_up.shape[0], q_mixed.shape[...  8.16 us
  transfers between devices with their start and end apart: 4, of which 3 were waited for; matrix products, arithmetic and copies ran while one was open for 7% of the time, Pallas kernels for 0%

profile of v1, /device:TPU:0, one launch (start us, length us, event | category | flops | bytes accessed | tf_op | source)
XLA Modules:
  0.0 368.6 jit_solution(7455243617888797985)
XLA Ops:
  6.5 0.7 all-gather.7.cloned.1.call-update
  7.3 0.7 all-gather.5.cloned.1.call-update
  8.0 59.2 %all-gather.7.cloned.1.call-done = bf16[8,4,32768]{2,1,0:T(4,128)(2,1)} async-done(((bf16[1,4,32768]{2,1,0:T(4,128)(2,1)}), bf16[8,4,32768]{2,1,0:T(4,128)(2,1)}) %all-gather.7.cloned.1.call-update) | async-done | bytes 2097168 | tf_op jit(solution)/shard_map/all_gather | solution.py:321
  67.2 3.3 all_to_all.27
  70.5 2.5 copy.69
  73.0 4.4 %all-to-all-start.1 = ((bf16[32,16,2048]{2,0,1:T(8,128)(2,1)}), bf16[32,16,2048]{2,0,1:T(8,128)(2,1)S(1)}, u32[]{:S(2)}, u32[]{:S(2)}) async-start(bf16[32,16,2048]{2,0,1:T(8,128)(2,1)} %copy.69), calls=%async_computation.1 | async-start | bytes 4194304 | tf_op jit(solution)/shard_map/all_to_all | solution.py:325
  77.4 101.9 %all-gather.5.cloned.1.call-done = bf16[8,12,24576]{2,1,0:T(8,128)(2,1)} async-done(((bf16[1,12,24576]{2,1,0:T(8,128)(2,1)}), bf16[8,12,24576]{2,1,0:T(8,128)(2,1)}) %all-gather.5.cloned.1.call-update) | async-done | bytes 4718608 | tf_op jit(solution)/shard_map/all_gather | solution.py:320
  179.4 8.7 %all_to_all.24 = bf16[96,16,1536]{2,1,0:T(8,128)(2,1)} reshape(bf16[8,12,24576]{2,1,0:T(8,128)(2,1)} %all-gather.5.cloned.1.call-done) | data formatting | bytes 9437184 | tf_op jit(solution)/shard_map/all_to_all | solution.py:324
  188.1 7.2 %copy.65 = bf16[96,16,1536]{2,0,1:T(8,128)(2,1)} copy(bf16[96,16,1536]{2,1,0:T(8,128)(2,1)} %all_to_all.24) | data formatting | bytes 9437184 | tf_op jit(solution)/shard_map/all_to_all | solution.py:324
  195.2 4.7 %all-to-all-start = ((bf16[96,16,1536]{2,0,1:T(8,128)(2,1)}), bf16[96,16,1536]{2,0,1:T(8,128)(2,1)}, u32[]{:S(2)}, u32[]{:S(2)}) async-start(bf16[96,16,1536]{2,0,1:T(8,128)(2,1)} %copy.65), calls=%async_computation | async-start | bytes 9437184 | tf_op jit(solution)/shard_map/all_to_all | solution.py:324
  200.0 7.7 %copy.78.cache_ref = bf16[8,512,576]{2,1,0:T(8,128)(2,1)} copy(bf16[8,512,576]{1,2,0:T(8,128)(2,1)} %param.9) | data formatting | bytes 9437184 | tf_op args[3]
  207.7 0.7 pad.4.new_ref
  208.5 0.3 multiply_cosine_fusion
  208.8 1.2 copy.70
  209.9 3.0 copy.71
  212.9 3.2 reshape_reshape.3
  216.1 0.1 fusion.3
  216.3 1.2 copy.91
  217.4 42.3 %all-to-all-done = bf16[96,16,1536]{2,0,1:T(8,128)(2,1)} async-done(((bf16[96,16,1536]{2,0,1:T(8,128)(2,1)}), bf16[96,16,1536]{2,0,1:T(8,128)(2,1)}, u32[]{:S(2)}, u32[]{:S(2)}) %all-to-all-start) | async-done | bytes 4718624 | tf_op jit(solution)/shard_map/all_to_all | solution.py:324
  259.7 4.9 %copy.66 = bf16[96,16,1536]{2,1,0:T(8,128)(2,1)S(1)} copy(bf16[96,16,1536]{2,0,1:T(8,128)(2,1)} %all-to-all-done) | data formatting | bytes 9437184 | tf_op jit(solution)/shard_map/all_to_all | solution.py:324
  264.6 5.6 %copy.67 = bf16[8,16,12,1536]{3,2,1,0:T(8,128)(2,1)} copy(bf16[8,16,12,1536]{3,1,2,0:T(8,128)(2,1)S(1)} %bitcast.36) | data formatting | bytes 9437184 | tf_op jit(solution)/shard_map/transpose | solution.py:329
  270.2 8.2 %reshape.78 = bf16[1536,1536]{1,0:T(8,128)(2,1)} reshape(bf16[8,16,12,1536]{3,2,1,0:T(8,128)(2,1)} %copy.67) | data formatting | bytes 9437184 | tf_op jit(solution)/shard_map/reshape | solution.py:330
  278.4 3.2 convolution_convert_fusion
  281.6 0.2 reshape.79
  281.8 0.3 copy.83
  282.3 0.3 subtract_convert_fusion
  282.7 0.4 copy.74
  283.1 0.5 fusion
  283.6 0.8 copy.80.own_ref
  284.4 0.7 broadcast_in_dim.2.len_ref
  285.1 75.2 %shard_map.64 = bf16[32,1024]{1,0:T(8,128)(2,1)} custom-call(bf16[8,32,576]{2,1,0:T(8,128)(2,1)} %copy.80.own_ref, bf16[8,512,576]{2,1,0:T(8,128)(2,1)} %copy.78.cache_ref, bf16[8,16,576]{2,1,0:T(8,128)(2,1)} %pad.4.new_ref, s32[8,512]{1,0:T(8,128)} %broadcast_in_dim.2.len_ref, bf16[8,512,128]{2,1,0:T(8,128)(2,1)} %bitcast.38), custom_call_target="tpu_custom_call" | custom-call | tf_op jit(solution)/shard_map/pallas_call | solution.py:277
  360.3 1.5 copy.94
  (17 shorter events, 0.4 us)
Async XLA Ops:
  6.5 271.9 %copy-start = (bf16[4,8,1536]{2,1,0:T(8,128)(2,1)S(1)}, bf16[4,8,1536]{2,1,0:T(8,128)(2,1)}, u32[]{:S(2)}) copy-start(bf16[4,8,1536]{2,1,0:T(8,128)(2,1)} %param.6) | copy-start | bytes 294916
  6.5 60.7 %all-gather.7.cloned.1.call-start = ((), (), s32[]{:S(2)}) async-start(), calls=%async_computation.3 | async-start | bytes 2359296 | tf_op jit(solution)/shard_map/all_gather | solution.py:321
  7.3 172.1 %all-gather.5.cloned.1.call-start = ((), (), s32[]{:S(2)}) async-start(), calls=%async_computation.2 | async-start | bytes 7077888 | tf_op jit(solution)/shard_map/all_gather | solution.py:320
  73.0 122.3 %all-to-all-start.1 = ((bf16[32,16,2048]{2,0,1:T(8,128)(2,1)}), bf16[32,16,2048]{2,0,1:T(8,128)(2,1)S(1)}, u32[]{:S(2)}, u32[]{:S(2)}) async-start(bf16[32,16,2048]{2,0,1:T(8,128)(2,1)} %copy.69), calls=%async_computation.1 | async-start | bytes 4194304 | tf_op jit(solution)/shard_map/all_to_all | solution.py:325
  195.2 64.5 %all-to-all-start = ((bf16[96,16,1536]{2,0,1:T(8,128)(2,1)}), bf16[96,16,1536]{2,0,1:T(8,128)(2,1)}, u32[]{:S(2)}, u32[]{:S(2)}) async-start(bf16[96,16,1536]{2,0,1:T(8,128)(2,1)} %copy.65), calls=%async_computation | async-start | bytes 9437184 | tf_op jit(solution)/shard_map/all_to_all | solution.py:324
  200.0 7.7 %copy-start.1 = (bf16[4,8,576]{2,1,0:T(8,128)(2,1)S(1)}, bf16[4,8,576]{2,1,0:T(8,128)(2,1)}, u32[]{:S(2)}) copy-start(bf16[4,8,576]{2,1,0:T(8,128)(2,1)} %param.10) | copy-start | bytes 110596
  200.0 8.4 %copy-start.2 = (s32[8]{0:T(128)S(1)}, s32[8]{0:T(128)}, u32[]{:S(2)}) copy-start(s32[8]{0:T(128)} %param.11) | copy-start | bytes 100
Sparse Core Ops, SparseCore 0:
  9.7 57.4 all-gather.6
  69.5 109.7 all-gather.4

commit v2 on v1

--- a/solution.py
+++ b/solution.py
@@ -1,5 +1,6 @@
 import jax
 import jax.numpy as jnp
+import numpy as np
 from jax import lax
 from jax.experimental import pallas as pl
 from jax.experimental.pallas import tpu as pltpu
@@ -15,38 +16,22 @@
 VDIM = 128
 STEPS = 4
 WIDTH = KVL + ROPE
+WIDE = KVL + 128
 LOG2E = 1.4426950408889634
-
-
-def rotate(pairs_in, position):
-    half = pairs_in.shape[-1] // 2
-    pairs = pairs_in.reshape(pairs_in.shape[:-1] + (half, 2))
-    freq = 10000.0 ** (-(2.0 * jnp.arange(half, dtype=jnp.float32)) / pairs_in.shape[-1])
-    angle = position[..., None] * freq
-    first = pairs[..., 0]
-    second = pairs[..., 1]
-    rotated = jnp.stack(
-        [
-            first * jnp.cos(angle) - second * jnp.sin(angle),
-            first * jnp.sin(angle) + second * jnp.cos(angle),
-        ],
-        -1,
-    )
-    return rotated.reshape(pairs_in.shape)
 
 
 class Copies:
     def __init__(self, send_sem, recv_sem):
         self.send_sem, self.recv_sem, self.sent = send_sem, recv_sem, []
 
-    def send(self, src, dst, peer):
+    def send(self, src, dst, peer, axis="grp"):
         k = len(self.sent)
         copy = pltpu.make_async_remote_copy(
             src_ref=src,
             dst_ref=dst,
             send_sem=self.send_sem.at[k],
             recv_sem=self.recv_sem.at[k],
-            device_id={"grp": peer},
+            device_id={axis: peer},
             device_id_type=MESH,
         )
         copy.start()
@@ -63,12 +48,14 @@
     return peak, a[1] * jnp.exp2(a[0] - peak) + b[1] * jnp.exp2(b[0] - peak)
 
 
-def attend_kernel(
-    own_ref, cache_ref, new_ref, len_ref, wv_ref, out_ref,
+def kernel(
+    ql_ref, q_ref, kv_ref, cache_ref, new_ref, len_ref, cos_ref, sin_ref, move_ref, out_ref,
+    X, LAND, QLS, W, KC, E, QR, WV,
     G, K, O, NB, RD, T, RF, RL, RR, RL1, RR1, RZ0, RZ1, U0, V1, M, L, ml_send, ml_recv, SC, SCT, F,
-    send_sem, recv_sem, cache_sem,
+    send_sem, recv_sem, cache_sem, all_send, all_recv,
 ):
-    gi = lax.axis_index("grp")
+    di, gi = lax.axis_index("dp"), lax.axis_index("grp")
+    me = di * 16 + gi
     x, zl, c = gi // 4, (gi // 2) % 2, gi % 2
     xp, xm, x2 = (x + 1) % 4, (x + 3) % 4, (x + 2) % 4
     zo, co = 1 - zl, 1 - c
@@ -82,12 +69,93 @@
     load = pltpu.make_async_copy(cache_ref, K, cache_sem)
     load.start()
     barrier = pltpu.get_barrier_semaphore()
-    for peer in (p_xp, p_xm, p_x2, p_z, p_c):
-        pl.semaphore_signal(barrier, inc=1, device_id={"grp": peer}, device_id_type=MESH)
-    G[:, pl.ds(gi, 1)] = own_ref[...][:, None]
-    pl.semaphore_wait(barrier, 5)
+
+    def there(j):
+        d = (me + 37 * j) % 128
+        return d // 16, d % 16
+
+    def greet(j, carry):
+        dd, gg = there(j)
+        pl.semaphore_signal(
+            barrier, inc=1, device_id={"dp": dd, "grp": gg}, device_id_type=MESH
+        )
+        return carry
+
+    lax.fori_loop(1, 128, greet, 0)
+
+    def pack(p, carry):
+        def tile(ref, n):
+            return ref[:, pl.ds(pl.multiple_of(n * 128, 128), 128)]
+
+        first, middle, last = tile(q_ref, 3 * p), tile(q_ref, 3 * p + 1), tile(q_ref, 3 * p + 2)
+        X[2 * p, 0:16] = first + tile(kv_ref, 4 * p)
+        X[2 * p, 16:32] = middle + tile(kv_ref, 4 * p + 1)
+        X[2 * p + 1, 0:16] = middle + tile(kv_ref, 4 * p + 2)
+        X[2 * p + 1, 16:32] = last + tile(kv_ref, 4 * p + 3)
+        return carry
+
+    lax.fori_loop(0, 64, pack, 0)
+    QLS[di, c] = ql_ref[c]
+    LAND[me] = X[8 * gi + di]
+    pl.semaphore_wait(barrier, 127)
 
     net = Copies(send_sem, recv_sem)
+    latents = [net.send(QLS.at[di, c], QLS.at[di, c], (di + j) % 8, "dp") for j in range(1, 8)]
+
+    def deal(j, carry):
+        dd, gg = there(j)
+        pltpu.make_async_remote_copy(
+            src_ref=X.at[8 * gg + dd],
+            dst_ref=LAND.at[me],
+            send_sem=all_send,
+            recv_sem=all_recv,
+            device_id={"dp": dd, "grp": gg},
+            device_id_type=MESH,
+        ).start()
+        return carry
+
+    lax.fori_loop(1, 128, deal, 0)
+    for copy in latents:
+        copy.wait_recv()
+    net.send(QLS.at[:, c], QLS.at[:, c], p_c).wait_recv()
+    pltpu.make_async_copy(LAND.at[0:127], LAND.at[0:127], all_recv).wait()
+
+    bf, f32 = jnp.bfloat16, jnp.float32
+    for b in range(16):
+        block = jnp.dot(
+            move_ref[0], LAND[8 * b : 8 * b + 8].reshape(256, 128), preferred_element_type=f32
+        ).astype(bf)
+        W[0, 96 * b : 96 * b + 96] = block[0:96]
+        W[1, 96 * b : 96 * b + 96] = block[96:192]
+        KC[32 * b : 32 * b + 32] = block[192:224]
+        WV[di, 32 * b : 32 * b + 32] = block[224:256]
+    latent_in = QLS[...].reshape(256, QL)
+    qa = jnp.dot(latent_in, W[0], preferred_element_type=f32)
+    qb = jnp.dot(latent_in, W[1], preferred_element_type=f32)
+    ra, rb = pltpu.roll(qa, 64, 1), pltpu.roll(qb, 64, 1)
+    lane = lax.broadcasted_iota(jnp.int32, (256, 128), 1)
+    odd = di % 2 == 1
+    plain = jnp.where(odd, jnp.where(lane < 64, ra, rb), qa).astype(bf)
+    rotary = jnp.where(lane < 64, jnp.where(odd, rb, qb), 0.0).astype(bf)
+    nt = (((1,), (1,)), ((), ()))
+    absorbed = lax.dot_general(plain, KC[...], nt, preferred_element_type=f32).astype(bf)
+    E[:, :, 0:KVL] = absorbed.reshape(8, 32, KVL)
+    E[:, :, KVL:WIDE] = rotary.reshape(8, 32, 128)
+    heads = []
+    for j in range(1, 8):
+        dd = (di + j) % 8
+        heads.append(net.send(E.at[dd], QR.at[di], dd, "dp"))
+    QR[di] = E[di]
+    for copy in heads:
+        copy.wait_recv()
+    values = [net.send(WV.at[di], WV.at[di], (di + j) % 8, "dp") for j in range(1, 8)]
+
+    turned = jnp.dot(move_ref[1], QR[...].reshape(256, WIDE), preferred_element_type=f32)
+    rotary = turned[:, KVL:]
+    other = jnp.where(lane % 2 == 0, pltpu.roll(rotary, 127, 1), pltpu.roll(rotary, 1, 1))
+    rotary = rotary * cos_ref[...] + other * sin_ref[...]
+    G[:, pl.ds(gi, 1), :, 0:KVL] = turned[:, :KVL].astype(bf).reshape(8, 1, 32, KVL)
+    G[:, pl.ds(gi, 1), :, KVL:WIDTH] = rotary[:, :ROPE].astype(bf).reshape(8, 1, 32, ROPE)
 
     def pass_on(first, count, slot, peer):
         block = G.at[pl.ds(first, count), slot]
@@ -161,14 +229,13 @@
     new_live = lax.broadcasted_iota(jnp.int32, (32, 16), 1) <= (
         lax.broadcasted_iota(jnp.int32, (32, 16), 0) % 4
     )
-    nt = (((1,), (1,)), ((), ()))
     rows = pl.ds(gi * 32, 32)
 
     def one_request(r, carry):
         q = G[r].reshape(512, WIDTH)
         k = K[r]
         kn = new_ref[r]
-        s = lax.dot_general(q, k, nt, preferred_element_type=jnp.float32) * to_log2
+        s = jnp.dot(q, k, preferred_element_type=jnp.float32) * to_log2
         s = jnp.where(key_at < len_ref[pl.ds(r, 1), :], s, -1e30)
         sn = lax.dot_general(G[r, gi], kn, nt, preferred_element_type=jnp.float32) * to_log2
         sn = jnp.where(new_live, sn, -1e30)
@@ -178,7 +245,9 @@
         pn = jnp.exp2(sn - M[rows, 0:1])
         L[...] = jnp.broadcast_to(jnp.sum(p, 1, keepdims=True), (512, 128))
         L[rows, :] = L[rows, :] + jnp.sum(pn, 1, keepdims=True)
-        O[r] = jnp.dot(p.astype(jnp.bfloat16), k[:, :KVL], preferred_element_type=jnp.float32)
+        O[r] = lax.dot_general(
+            p.astype(jnp.bfloat16), k[:KVL], nt, preferred_element_type=jnp.float32
+        )
         O[r, rows, :] = O[r, rows, :] + jnp.dot(
             pn.astype(jnp.bfloat16), kn[:, :KVL], preferred_element_type=jnp.float32
         )
@@ -255,33 +324,68 @@
         V1[:, x].astype(jnp.float32) + RL1[...].astype(jnp.float32) + RR1[...].astype(jnp.float32)
     ).astype(jnp.bfloat16)
 
-    to = lax.broadcasted_iota(jnp.int32, (256, 256), 0)
-    was = lax.broadcasted_iota(jnp.int32, (256, 256), 1)
-    move = (was == (to % 8) * 32 + to // 8).astype(jnp.bfloat16)
     latent = jnp.dot(
-        move, F[...].reshape(256, KVL), preferred_element_type=jnp.float32
+        move_ref[2], F[...].reshape(256, KVL), preferred_element_type=jnp.float32
     ).astype(jnp.bfloat16)
+    for copy in values:
+        copy.wait_recv()
     for i in range(8):
         out_ref[:, i * VDIM : (i + 1) * VDIM] = jnp.dot(
-            latent[i * 32 : (i + 1) * 32], wv_ref[i], preferred_element_type=jnp.float32
+            latent[i * 32 : (i + 1) * 32], WV[i], preferred_element_type=jnp.float32
         ).astype(jnp.bfloat16)
     net.finish()
-
-
-def attend(own, cache, new_latent, lengths, w_value):
+    pltpu.make_async_copy(X.at[0:127], X.at[0:127], all_send).wait()
+
+
+def moves():
+    sources = np.arange(256).reshape(8, 32)
+    deal = np.concatenate(
+        [sources[:, a:b].reshape(-1) for a, b in ((0, 12), (16, 28), (12, 16), (28, 32))]
+    )
+    turn = np.arange(256).reshape(8, 4, 8).transpose(2, 0, 1).reshape(-1)
+    back = np.arange(256).reshape(8, 8, 4).transpose(1, 2, 0).reshape(-1)
+    return np.stack([np.eye(256)[order] for order in (deal, turn, back)])
+
+
+def rotation(lengths):
+    freq = 10000.0 ** (-(2.0 * jnp.arange(ROPE // 2, dtype=jnp.float32)) / ROPE)
+    position = (lengths[:, None] + jnp.arange(STEPS, dtype=jnp.int32)).astype(jnp.float32)
+    angle = position[..., None] * jnp.repeat(freq, 2)
+    sign = jnp.where(jnp.arange(ROPE) % 2 == 0, -1.0, 1.0)
+
+    def rows(table):
+        table = jnp.pad(table, ((0, 0), (0, 0), (0, 128 - ROPE)))
+        return jnp.broadcast_to(table[:, None], (8, 8, STEPS, 128)).reshape(256, 128)
+
+    return rows(jnp.cos(angle)), rows(jnp.sin(angle) * sign)
+
+
+def per_device(query_latent, q_up, kv_up, latent_cache, new_latent, lengths):
+    bf, f32 = jnp.bfloat16, jnp.float32
+    latent_in = query_latent.reshape(2, 16, QL)
+    q_rows = jnp.pad(q_up, ((0, 4), (0, 0)))
+    kv_rows = jnp.pad(kv_up, ((12, 0), (0, 0)))
     fresh = jnp.pad(new_latent.transpose(1, 0, 2), ((0, 0), (0, 16 - STEPS), (0, 0)))
     limit = jnp.broadcast_to(lengths[:, None], (8, 512))
+    cosines, sines = rotation(lengths)
     vmem = pl.BlockSpec(memory_space=pltpu.VMEM)
-    bf, f32 = jnp.bfloat16, jnp.float32
-    copies = 64
-    return pl.pallas_call(
-        attend_kernel,
+    copies = 96
+    out = pl.pallas_call(
+        kernel,
         out_shape=jax.ShapeDtypeStruct((32, 8 * VDIM), bf),
-        in_specs=[vmem, pl.BlockSpec(memory_space=pl.ANY), vmem, vmem, vmem],
+        in_specs=[vmem] * 3 + [pl.BlockSpec(memory_space=pl.ANY)] + [vmem] * 5,
         out_specs=vmem,
         scratch_shapes=[
+            pltpu.VMEM((128, 32, 128), bf),
+            pltpu.VMEM((128, 32, 128), bf),
+            pltpu.VMEM((8, 2, 16, QL), bf),
+            pltpu.VMEM((2, QL, 128), bf),
+            pltpu.VMEM((KVL, NOPE), bf),
+            pltpu.VMEM((8, 32, WIDE), bf),
+            pltpu.VMEM((8, 32, WIDE), bf),
+            pltpu.VMEM((8, KVL, VDIM), bf),
             pltpu.VMEM((8, 16, 32, WIDTH), bf),
-            pltpu.VMEM((8, 512, WIDTH), bf),
+            pltpu.VMEM((8, WIDTH, 512), bf),
             pltpu.VMEM((8, 512, KVL), f32),
             pltpu.VMEM((8, 4, 2, 2, 32, KVL), bf),
             pltpu.VMEM((8, 4, 2, 32, KVL), bf),
@@ -305,51 +409,17 @@
             pltpu.SemaphoreType.DMA((copies,)),
             pltpu.SemaphoreType.DMA((copies,)),
             pltpu.SemaphoreType.DMA,
+            pltpu.SemaphoreType.DMA,
+            pltpu.SemaphoreType.DMA,
         ],
         compiler_params=pltpu.CompilerParams(
-            collective_id=1, has_side_effects=True, vmem_limit_bytes=56 * 1024 * 1024
+            collective_id=1, has_side_effects=True, vmem_limit_bytes=60 * 1024 * 1024
         ),
-    )(own, cache, fresh, limit, w_value)
-
-
-def per_device(query_latent, q_up, kv_up, latent_cache, new_latent, lengths):
-    groups = lax.axis_size("grp")
-    replicas = lax.axis_size("dp")
-    heads = H // groups
-    q_rows, kv_rows = (
-        lax.all_gather(q_up, "dp", axis=0, tiled=True),
-        lax.all_gather(kv_up, "dp", axis=0, tiled=True),
+    )(
+        latent_in, q_rows, kv_rows, latent_cache.transpose(0, 2, 1), fresh, limit, cosines, sines,
+        jnp.asarray(moves(), bf),
     )
-    q_mixed, kv_mixed = (
-        lax.all_to_all(q_rows, "grp", split_axis=1, concat_axis=0, tiled=True),
-        lax.all_to_all(kv_rows, "grp", split_axis=1, concat_axis=0, tiled=True),
-    )
-    q_owned = (
-        q_mixed.reshape(groups, replicas, q_up.shape[0], q_mixed.shape[1])
-        .transpose(1, 0, 2, 3)
-        .reshape(QL, q_mixed.shape[1])
-    )
-    kv_owned = (
-        kv_mixed.reshape(groups, replicas, kv_up.shape[0], kv_mixed.shape[1])
-        .transpose(1, 0, 2, 3)
-        .reshape(KVL, kv_mixed.shape[1])
-    )
-    requests = query_latent.shape[1]
-    q = jnp.dot(
-        query_latent.reshape(STEPS * requests, QL), q_owned, preferred_element_type=jnp.float32
-    )
-    q = q.astype(jnp.bfloat16).reshape(STEPS, requests, heads, NOPE + ROPE)
-    blocks = kv_owned.reshape(KVL, heads, NOPE + VDIM)
-    w_key = blocks[:, :, :NOPE]
-    w_value = blocks[:, :, NOPE:]
-    q_abs = jnp.einsum("srhd,chd->srhc", q[..., :NOPE], w_key, preferred_element_type=jnp.float32)
-    step_ids = lax.broadcasted_iota(jnp.int32, (STEPS, 1), 0)
-    position = (lengths[None, :] + step_ids).astype(jnp.float32)
-    q_rot = rotate(q[..., NOPE:].astype(jnp.float32), position[:, :, None])
-    q_cat = jnp.concatenate([q_abs, q_rot], -1).astype(jnp.bfloat16)
-    own = q_cat.transpose(1, 2, 0, 3).reshape(requests, heads * STEPS, WIDTH)
-    out = attend(own, latent_cache, new_latent, lengths, w_value.transpose(1, 0, 2))
-    return out.reshape(STEPS, requests, heads * VDIM)
+    return out.reshape(STEPS, 8, 8 * VDIM)
 
 
 def solution(mesh):

time: 371 us -> 126 us (0.34)
  waiting for transfers between devices: 205 us -> 0 us
  local copies, waits for them, and re-layouts: 61.2 us -> 10.1 us
  Pallas kernels: 75.2 us -> 113 us
  between operations: 13.6 us -> 0.04 us
  starting transfers between devices: 9.22 us -> 0 us
    all_gather x2 -> x0, waiting for transfers between devices: 161 us -> none  [the longest x1 102 us: per_device(): lax.all_gather(q_up, 'dp', axis=0, tiled=True)]
    all_to_all x2 -> x0, waiting for transfers between devices: 42.3 us -> none  [the longest x1 42.3 us: per_device(): lax.all_to_all(q_rows, 'grp', split_axis=1, concat_axis=0, tiled=True)]
    pallas_call x1, Pallas kernels: 75.2 us -> 113 us  [per_device(): pl.pallas_call(kernel, out_shape=jax.ShapeDtypeStruct((32, 8 * VDIM), bf)...]
    all_to_all x6 -> x0, local copies, waits for them, and re-layouts: 27.7 us -> none  [the longest x3 20.8 us: per_device(): lax.all_to_all(q_rows, 'grp', split_axis=1, concat_axis=0, tiled=True)]
    reshape x4 -> x0, local copies, waits for them, and re-layouts: 9.48 us -> none  [the longest x1 8.16 us: per_device(): q_owned = q_mixed.reshape(groups, replicas, q_up.shape[0], q_mixed.shape[...]
    all_to_all x2 -> x0, starting transfers between devices: 9.18 us -> none  [the longest x1 4.73 us: per_device(): lax.all_to_all(q_rows, 'grp', split_axis=1, concat_axis=0, tiled=True)]
    transpose x2 -> x0, local copies, waits for them, and re-layouts: 8.58 us -> none  [the longest x1 5.61 us: per_device(): q_owned = q_mixed.reshape(groups, replicas, q_up.shape[0], q_mixed.shape[...]
    unnamed x11 -> x2, local copies, waits for them, and re-layouts: 10.7 us -> 2.27 us
  transfers between devices with their start and end apart: 4 -> 0, of which waited for: 3 -> 0; matrix products, arithmetic and copies ran while one was open for 7% -> 0% of each run, Pallas kernels for 0% -> 0%
where the time goes in v2:
time: 126 us; the launch traced here: 124 us
  Pallas kernels  113 us (90%)
  local copies, waits for them, and re-layouts  10.1 us (8%)
    pallas_call x1, Pallas kernels, per_device(): pl.pallas_call(kernel, out_shape=jax.ShapeDtypeStruct((32, 8 * VDIM), bf)...  113 us

profile of v2, /device:TPU:0, one launch (start us, length us, event | category | flops | bytes accessed | tf_op | source)
XLA Modules:
  0.0 124.1 jit_solution(17855312537099741542)
XLA Ops:
  0.0 0.7 add_convert_fusion
  0.7 0.1 broadcast_in_dim.17
  0.8 0.1 mul.32
  0.9 1.3 %broadcast_in_dim.16.len_ref = s32[8,512]{1,0:T(8,128)} broadcast(s32[8]{0:T(128)} %param.12), dimensions={0} | broadcast | bytes 16416 | tf_op jit(solution)/shard_map/broadcast_in_dim | solution.py:369
  2.3 0.2 fusion
  2.5 0.8 copy.11
  3.3 0.7 broadcast_in_dim.18
  3.9 0.7 broadcast_in_dim.38
  4.6 0.7 pad.21.new_ref
  5.3 2.1 %pad.19.q_ref = bf16[16,24576]{1,0:T(8,128)(2,1)} pad(bf16[12,24576]{1,0:T(8,128)(2,1)} %param.8, bf16[]{:T(256)} %constant.25.clone.1), padding=0_4x0_0 | pad | bytes 1376258 | tf_op jit(solution)/shard_map/jit(_pad)/pad | solution.py:366
  7.4 2.1 %pad.20.kv_ref = bf16[16,32768]{1,0:T(8,128)(2,1)} pad(bf16[4,32768]{1,0:T(4,128)(2,1)} %param.9, bf16[]{:T(256)} %constant.25.clone.1), padding=12_0x0_0 | pad | bytes 1310722 | tf_op jit(solution)/shard_map/jit(_pad)/pad | solution.py:367
  9.6 113.1 %shard_map.73 = bf16[32,1024]{1,0:T(8,128)(2,1)} custom-call(bf16[2,16,1536]{2,1,0:T(8,128)(2,1)} %bitcast.13, bf16[16,24576]{1,0:T(8,128)(2,1)} %pad.19.q_ref, bf16[16,32768]{1,0:T(8,128)(2,1)} %pad.20.kv_ref, bf16[8,576,512]{2,1,0:T(8,128)(2,1)} %bitcast.8, bf16[8,16,576]{2,1,0:T(8,128)(2,1)} %pad.21.new_ref, s32[8,512]{1,0:T(8,128)} %broadcast_in_dim.16.len_ref, ...), custom_call_target="tpu_custom_call" | custom-call | tf_op jit(solution)/shard_map/pallas_call | solution.py:373
  122.7 1.5 %copy.13 = bf16[4,8,1024]{2,1,0:T(8,128)(2,1)} copy(bf16[4,8,1024]{2,1,0:T(8,128)(2,1)} %bitcast.11) | data formatting | bytes 131072
  (4 shorter events, 0.0 us)

commit v3 on v2

--- a/solution.py
+++ b/solution.py
@@ -49,10 +49,10 @@
 
 
 def kernel(
-    ql_ref, q_ref, kv_ref, cache_ref, new_ref, len_ref, cos_ref, sin_ref, move_ref, out_ref,
-    X, LAND, QLS, W, KC, E, QR, WV,
+    len_ref, freq_ref, ql_ref, q_ref, kv_ref, cache_ref, new_ref, out_ref,
+    QIN, KVIN, NEW, MOVE, SN, X, LAND, QLS, W, KC, E, QR, WV,
     G, K, O, NB, RD, T, RF, RL, RR, RL1, RR1, RZ0, RZ1, U0, V1, M, L, ml_send, ml_recv, SC, SCT, F,
-    send_sem, recv_sem, cache_sem, all_send, all_recv,
+    send_sem, recv_sem, load_sem, all_send, all_recv,
 ):
     di, gi = lax.axis_index("dp"), lax.axis_index("grp")
     me = di * 16 + gi
@@ -66,8 +66,12 @@
     p_xp, p_xm, p_x2 = at(xp, zl, c), at(xm, zl, c), at(x2, zl, c)
     p_z, p_c = at(x, zo, c), at(x, zl, co)
 
-    load = pltpu.make_async_copy(cache_ref, K, cache_sem)
-    load.start()
+    loads = [
+        pltpu.make_async_copy(src, dst, load_sem.at[n])
+        for n, (src, dst) in enumerate(
+            ((q_ref, QIN), (kv_ref, KVIN), (ql_ref.at[c], QLS.at[di, c]), (new_ref, NEW), (cache_ref, K))
+        )
+    ]
     barrier = pltpu.get_barrier_semaphore()
 
     def there(j):
@@ -83,20 +87,40 @@
 
     lax.fori_loop(1, 128, greet, 0)
 
+    for load in loads:
+        load.start()
+    bf, f32 = jnp.bfloat16, jnp.float32
+    nt = (((1,), (1,)), ((), ()))
+
+    to = lax.broadcasted_iota(jnp.int32, (256, 256), 0)
+    was = lax.broadcasted_iota(jnp.int32, (256, 256), 1)
+    within = jnp.where(to < 96, to, to - 96)
+    twelve = jnp.where(to < 96, to, to - 80)
+    for n in range(1, 8):
+        twelve = twelve + jnp.where(within >= 12 * n, 20, 0)
+    four = 32 * ((to % 32) // 4) + to % 4 + jnp.where(to < 224, 12, 28)
+    MOVE[0] = (was == jnp.where(to < 192, twelve, four)).astype(f32).astype(bf)
+    MOVE[1] = (was == ((to // 4) % 8) * 32 + (to % 4) * 8 + to // 32).astype(f32).astype(bf)
+    MOVE[2] = (was == (to % 8) * 32 + to // 8).astype(f32).astype(bf)
+
+    loads[0].wait()
+    loads[1].wait()
+
     def pack(p, carry):
-        def tile(ref, n):
-            return ref[:, pl.ds(pl.multiple_of(n * 128, 128), 128)]
-
-        first, middle, last = tile(q_ref, 3 * p), tile(q_ref, 3 * p + 1), tile(q_ref, 3 * p + 2)
-        X[2 * p, 0:16] = first + tile(kv_ref, 4 * p)
-        X[2 * p, 16:32] = middle + tile(kv_ref, 4 * p + 1)
-        X[2 * p + 1, 0:16] = middle + tile(kv_ref, 4 * p + 2)
-        X[2 * p + 1, 16:32] = last + tile(kv_ref, 4 * p + 3)
+        def tiles(upper, lower):
+            a = QIN[:, pl.ds(pl.multiple_of(upper * 128, 128), 128)]
+            b = KVIN[:, pl.ds(pl.multiple_of(lower * 128, 128), 128)]
+            return jnp.concatenate([a, b], 0)
+
+        X[2 * p, 0:16] = tiles(3 * p, 4 * p)
+        X[2 * p, 16:32] = tiles(3 * p + 1, 4 * p + 1)
+        X[2 * p + 1, 0:16] = tiles(3 * p + 1, 4 * p + 2)
+        X[2 * p + 1, 16:32] = tiles(3 * p + 2, 4 * p + 3)
         return carry
 
     lax.fori_loop(0, 64, pack, 0)
-    QLS[di, c] = ql_ref[c]
     LAND[me] = X[8 * gi + di]
+    loads[2].wait()
     pl.semaphore_wait(barrier, 127)
 
     net = Copies(send_sem, recv_sem)
@@ -115,15 +139,23 @@
         return carry
 
     lax.fori_loop(1, 128, deal, 0)
+
+    row = lax.broadcasted_iota(jnp.int32, (32, 128), 0)
+    lane32 = lax.broadcasted_iota(jnp.int32, (32, 128), 1)
+    position = row // 8
+    for r in range(8):
+        position = position + jnp.where(row % 8 == r, len_ref[r], 0)
+    angle = position.astype(f32) * freq_ref[...]
+    cosine = jnp.cos(angle)
+    sine = jnp.where(lane32 % 2 == 0, -1.0, 1.0) * jnp.sin(angle)
     for copy in latents:
         copy.wait_recv()
     net.send(QLS.at[:, c], QLS.at[:, c], p_c).wait_recv()
     pltpu.make_async_copy(LAND.at[0:127], LAND.at[0:127], all_recv).wait()
 
-    bf, f32 = jnp.bfloat16, jnp.float32
     for b in range(16):
         block = jnp.dot(
-            move_ref[0], LAND[8 * b : 8 * b + 8].reshape(256, 128), preferred_element_type=f32
+            MOVE[0], LAND[8 * b : 8 * b + 8].reshape(256, 128), preferred_element_type=f32
         ).astype(bf)
         W[0, 96 * b : 96 * b + 96] = block[0:96]
         W[1, 96 * b : 96 * b + 96] = block[96:192]
@@ -137,7 +169,6 @@
     odd = di % 2 == 1
     plain = jnp.where(odd, jnp.where(lane < 64, ra, rb), qa).astype(bf)
     rotary = jnp.where(lane < 64, jnp.where(odd, rb, qb), 0.0).astype(bf)
-    nt = (((1,), (1,)), ((), ()))
     absorbed = lax.dot_general(plain, KC[...], nt, preferred_element_type=f32).astype(bf)
     E[:, :, 0:KVL] = absorbed.reshape(8, 32, KVL)
     E[:, :, KVL:WIDE] = rotary.reshape(8, 32, 128)
@@ -150,11 +181,14 @@
         copy.wait_recv()
     values = [net.send(WV.at[di], WV.at[di], (di + j) % 8, "dp") for j in range(1, 8)]
 
-    turned = jnp.dot(move_ref[1], QR[...].reshape(256, WIDE), preferred_element_type=f32)
-    rotary = turned[:, KVL:]
+    rotary = QR[:, :, KVL:WIDE].reshape(256, 128).astype(f32)
     other = jnp.where(lane % 2 == 0, pltpu.roll(rotary, 127, 1), pltpu.roll(rotary, 1, 1))
-    rotary = rotary * cos_ref[...] + other * sin_ref[...]
-    G[:, pl.ds(gi, 1), :, 0:KVL] = turned[:, :KVL].astype(bf).reshape(8, 1, 32, KVL)
+    rotary = (
+        rotary.reshape(8, 32, 128) * cosine[None] + other.reshape(8, 32, 128) * sine[None]
+    ).reshape(256, 128)
+    absorbed = jnp.dot(MOVE[1], QR[:, :, 0:KVL].reshape(256, KVL), preferred_element_type=f32)
+    rotary = jnp.dot(MOVE[1], rotary.astype(bf), preferred_element_type=f32)
+    G[:, pl.ds(gi, 1), :, 0:KVL] = absorbed.astype(bf).reshape(8, 1, 32, KVL)
     G[:, pl.ds(gi, 1), :, KVL:WIDTH] = rotary[:, :ROPE].astype(bf).reshape(8, 1, 32, ROPE)
 
     def pass_on(first, count, slot, peer):
@@ -221,24 +255,27 @@
     mate.append(pass_on(6, 2, s_fz, p_c))
     for copy in mate:
         copy.wait_recv()
-    load.wait()
+    loads[4].wait()
 
     to_log2 = float(NOPE + ROPE) ** -0.5 * LOG2E
     lane = lax.broadcasted_iota(jnp.int32, (512, 128), 1)
     key_at = lax.broadcasted_iota(jnp.int32, (1, 512), 1) + gi * 512
-    new_live = lax.broadcasted_iota(jnp.int32, (32, 16), 1) <= (
-        lax.broadcasted_iota(jnp.int32, (32, 16), 0) % 4
+    loads[3].wait()
+    query = lax.broadcasted_iota(jnp.int32, (256, 32), 0)
+    key = lax.broadcasted_iota(jnp.int32, (256, 32), 1)
+    new_live = (key % 8 == query // 32) & (key // 8 <= query % 4)
+    new_score = lax.dot_general(
+        G[:, pl.ds(gi, 1)].reshape(256, WIDTH), NEW[...], nt, preferred_element_type=f32
     )
+    SN[...] = jnp.where(new_live, new_score * to_log2, -1e30)
     rows = pl.ds(gi * 32, 32)
 
     def one_request(r, carry):
         q = G[r].reshape(512, WIDTH)
         k = K[r]
-        kn = new_ref[r]
         s = jnp.dot(q, k, preferred_element_type=jnp.float32) * to_log2
-        s = jnp.where(key_at < len_ref[pl.ds(r, 1), :], s, -1e30)
-        sn = lax.dot_general(G[r, gi], kn, nt, preferred_element_type=jnp.float32) * to_log2
-        sn = jnp.where(new_live, sn, -1e30)
+        s = jnp.where(key_at < len_ref[r], s, -1e30)
+        sn = SN[pl.ds(r * 32, 32), :]
         M[...] = jnp.broadcast_to(jnp.maximum(jnp.max(s, 1, keepdims=True), -1e29), (512, 128))
         M[rows, :] = jnp.maximum(M[rows, :], jnp.max(sn, 1, keepdims=True))
         p = jnp.exp2(s - M[:, 0:1])
@@ -249,7 +286,7 @@
             p.astype(jnp.bfloat16), k[:KVL], nt, preferred_element_type=jnp.float32
         )
         O[r, rows, :] = O[r, rows, :] + jnp.dot(
-            pn.astype(jnp.bfloat16), kn[:, :KVL], preferred_element_type=jnp.float32
+            pn.astype(jnp.bfloat16), NEW[:, :KVL], preferred_element_type=jnp.float32
         )
         both = jnp.transpose(jnp.where(lane == 0, M[...], L[...]))
         ml_send[0, 0, pl.ds(r, 1), :] = both[0:1]
@@ -325,7 +362,7 @@
     ).astype(jnp.bfloat16)
 
     latent = jnp.dot(
-        move_ref[2], F[...].reshape(256, KVL), preferred_element_type=jnp.float32
+        MOVE[2], F[...].reshape(256, KVL), preferred_element_type=jnp.float32
     ).astype(jnp.bfloat16)
     for copy in values:
         copy.wait_recv()
@@ -337,45 +374,23 @@
     pltpu.make_async_copy(X.at[0:127], X.at[0:127], all_send).wait()
 
 
-def moves():
-    sources = np.arange(256).reshape(8, 32)
-    deal = np.concatenate(
-        [sources[:, a:b].reshape(-1) for a, b in ((0, 12), (16, 28), (12, 16), (28, 32))]
-    )
-    turn = np.arange(256).reshape(8, 4, 8).transpose(2, 0, 1).reshape(-1)
-    back = np.arange(256).reshape(8, 8, 4).transpose(1, 2, 0).reshape(-1)
-    return np.stack([np.eye(256)[order] for order in (deal, turn, back)])
-
-
-def rotation(lengths):
-    freq = 10000.0 ** (-(2.0 * jnp.arange(ROPE // 2, dtype=jnp.float32)) / ROPE)
-    position = (lengths[:, None] + jnp.arange(STEPS, dtype=jnp.int32)).astype(jnp.float32)
-    angle = position[..., None] * jnp.repeat(freq, 2)
-    sign = jnp.where(jnp.arange(ROPE) % 2 == 0, -1.0, 1.0)
-
-    def rows(table):
-        table = jnp.pad(table, ((0, 0), (0, 0), (0, 128 - ROPE)))
-        return jnp.broadcast_to(table[:, None], (8, 8, STEPS, 128)).reshape(256, 128)
-
-    return rows(jnp.cos(angle)), rows(jnp.sin(angle) * sign)
-
-
 def per_device(query_latent, q_up, kv_up, latent_cache, new_latent, lengths):
     bf, f32 = jnp.bfloat16, jnp.float32
-    latent_in = query_latent.reshape(2, 16, QL)
-    q_rows = jnp.pad(q_up, ((0, 4), (0, 0)))
-    kv_rows = jnp.pad(kv_up, ((12, 0), (0, 0)))
-    fresh = jnp.pad(new_latent.transpose(1, 0, 2), ((0, 0), (0, 16 - STEPS), (0, 0)))
-    limit = jnp.broadcast_to(lengths[:, None], (8, 512))
-    cosines, sines = rotation(lengths)
+    pair = np.arange(128) // 2
+    freq = np.where(pair < ROPE // 2, 10000.0 ** (-(2.0 * pair) / ROPE), 0.0).astype(np.float32)
     vmem = pl.BlockSpec(memory_space=pltpu.VMEM)
     copies = 96
     out = pl.pallas_call(
         kernel,
         out_shape=jax.ShapeDtypeStruct((32, 8 * VDIM), bf),
-        in_specs=[vmem] * 3 + [pl.BlockSpec(memory_space=pl.ANY)] + [vmem] * 5,
+        in_specs=[pl.BlockSpec(memory_space=pltpu.SMEM), vmem] + [pl.BlockSpec(memory_space=pl.ANY)] * 5,
         out_specs=vmem,
         scratch_shapes=[
+            pltpu.VMEM((12, H * (NOPE + ROPE)), bf),
+            pltpu.VMEM((4, H * (NOPE + VDIM)), bf),
+            pltpu.VMEM((32, WIDTH), bf),
+            pltpu.VMEM((3, 256, 256), bf),
+            pltpu.VMEM((256, 32), f32),
             pltpu.VMEM((128, 32, 128), bf),
             pltpu.VMEM((128, 32, 128), bf),
             pltpu.VMEM((8, 2, 16, QL), bf),
@@ -408,7 +423,7 @@
             pltpu.VMEM((8, 32, KVL), bf),
             pltpu.SemaphoreType.DMA((copies,)),
             pltpu.SemaphoreType.DMA((copies,)),
-            pltpu.SemaphoreType.DMA,
+            pltpu.SemaphoreType.DMA((5,)),
             pltpu.SemaphoreType.DMA,
             pltpu.SemaphoreType.DMA,
         ],
@@ -416,8 +431,8 @@
             collective_id=1, has_side_effects=True, vmem_limit_bytes=60 * 1024 * 1024
         ),
     )(
-        latent_in, q_rows, kv_rows, latent_cache.transpose(0, 2, 1), fresh, limit, cosines, sines,
-        jnp.asarray(moves(), bf),
+        lengths, jnp.asarray(freq)[None], query_latent.reshape(2, 16, QL), q_up, kv_up,
+        latent_cache.transpose(0, 2, 1), new_latent.reshape(32, WIDTH),
     )
     return out.reshape(STEPS, 8, 8 * VDIM)
 

time: 126 us -> 116 us (0.921)
  local copies, waits for them, and re-layouts: 10.1 us -> 1.47 us
    pad x5 -> x0, local copies, waits for them, and re-layouts: 4.94 us -> none  [the longest x1 2.12 us: per_device(): q_rows = jnp.pad(q_up, ((0, 4), (0, 0)))]
    broadcast_in_dim x4 -> x0, local copies, waits for them, and re-layouts: 2.75 us -> none  [the longest x2 1.35 us: rows(): jnp.broadcast_to(table[:, None], (8, 8, STEPS, 128)).reshape(256, 128)]
where the time goes in v3:
time: 116 us; the launch traced here: 114 us
  Pallas kernels  113 us (97%)
  local copies, waits for them, and re-layouts  1.47 us (1%)
    pallas_call x1, Pallas kernels, per_device(): pl.pallas_call(kernel, out_shape=jax.ShapeDtypeStruct((32, 8 * VDIM), bf)...  113 us

profile of v3, /device:TPU:0, one launch (start us, length us, event | category | flops | bytes accessed | tf_op | source)
XLA Modules:
  0.0 114.2 jit_solution(17080624852637115952)
XLA Ops:
  0.0 112.7 %shard_map.73 = bf16[32,1024]{1,0:T(8,128)(2,1)} custom-call(s32[8]{0:T(128)} %len_ref.1, f32[1,128]{1,0:T(1,128)} %constant.5.freq_ref, bf16[2,16,1536]{2,1,0:T(8,128)(2,1)} %bitcast.6, bf16[12,24576]{1,0:T(8,128)(2,1)} %q_ref.1, bf16[4,32768]{1,0:T(4,128)(2,1)} %kv_ref.1, bf16[8,576,512]{2,1,0:T(8,128)(2,1)} %bitcast.4, bf16[32,576]{1,0:T(8,128)(2,1)} %bitcast.7), custom_call_target="tpu_custom_call" | custom-call | tf_op jit(solution)/shard_map/pallas_call | solution.py:383
  112.7 1.5 %copy.9 = bf16[4,8,1024]{2,1,0:T(8,128)(2,1)} copy(bf16[4,8,1024]{2,1,0:T(8,128)(2,1)} %bitcast.5) | data formatting | bytes 131072

commit v4 on v3

v4 whole, which is shorter than its diff:
```python
import jax
import jax.numpy as jnp
import numpy as np
from jax import lax
from jax.experimental import pallas as pl
from jax.experimental.pallas import tpu as pltpu
from jax.sharding import PartitionSpec as P

MESH = pl.DeviceIdType.MESH

H = 128
QL = 1536
KVL = 512
NOPE = 128
ROPE = 64
VDIM = 128
STEPS = 4
WIDTH = KVL + ROPE
WIDE = KVL + 128
LOG2E = 1.4426950408889634


class Copies:
    def __init__(self, send_sem, recv_sem):
        self.send_sem, self.recv_sem, self.sent = send_sem, recv_sem, []

    def send(self, src, dst, peer, axis="grp"):
        k = len(self.sent)
        copy = pltpu.make_async_remote_copy(
            src_ref=src,
            dst_ref=dst,
            send_sem=self.send_sem.at[k],
            recv_sem=self.recv_sem.at[k],
            device_id={axis: peer},
            device_id_type=MESH,
        )
        copy.start()
        self.sent.append(copy)
        return copy

    def finish(self):
        for copy in self.sent:
            copy.wait_send()


def merge(a, b):
    peak = jnp.maximum(a[0], b[0])
    return peak, a[1] * jnp.exp2(a[0] - peak) + b[1] * jnp.exp2(b[0] - peak)


def kernel(
    len_ref, freq_ref, ql_ref, q_ref, kv_ref, cache_ref, new_ref, out_ref,
    QIN, KVIN, NEW, MOVE, SN, X, LAND, QLS, W, KC, E, QR, WV,
    G, K, O, NB, RD, T, V, U, RFA, RLA, RRA, RZA, RFB, RLB, RRB, RZB, M, L, ml_send, ml_recv, SC, SCT, F,
    send_sem, recv_sem, load_sem, all_send, all_recv,
):
    di, gi = lax.axis_index("dp"), lax.axis_index("grp")
    me = di * 16 + gi
    x, zl, c = gi // 4, (gi // 2) % 2, gi % 2
    xp, xm, x2 = (x + 1) % 4, (x + 3) % 4, (x + 2) % 4
    zo, co = 1 - zl, 1 - c

    def at(xx, zz, cc):
        return xx * 4 + zz * 2 + cc

    p_xp, p_xm, p_x2 = at(xp, zl, c), at(xm, zl, c), at(x2, zl, c)
    p_z, p_c = at(x, zo, c), at(x, zl, co)

    loads = [
        pltpu.make_async_copy(src, dst, load_sem.at[n])
        for n, (src, dst) in enumerate(
            ((q_ref, QIN), (kv_ref, KVIN), (ql_ref, QLS.at[0]), (new_ref, NEW), (cache_ref, K))
        )
    ]
    for load in loads:
        load.start()
    barrier = pltpu.get_barrier_semaphore()

    def there(j):
        d = (me + 37 * j) % 128
        return d // 16, d % 16

    def greet(j, carry):
        dd, gg = there(j)
        pl.semaphore_signal(
            barrier, inc=1, device_id={"dp": dd, "grp": gg}, device_id_type=MESH
        )
        return carry

    lax.fori_loop(1, 128, greet, 0)
    bf, f32 = jnp.bfloat16, jnp.float32
    nt = (((1,), (1,)), ((), ()))

    loads[0].wait()
    loads[1].wait()

    def pack(p, carry):
        def tiles(upper, lower):
            a = QIN[:, pl.ds(pl.multiple_of(upper * 128, 128), 128)]
            b = KVIN[:, pl.ds(pl.multiple_of(lower * 128, 128), 128)]
            return jnp.concatenate([a, b], 0)

        X[2 * p, 0:16] = tiles(3 * p, 4 * p)
        X[2 * p, 16:32] = tiles(3 * p + 1, 4 * p + 1)
        X[2 * p + 1, 0:16] = tiles(3 * p + 1, 4 * p + 2)
        X[2 * p + 1, 16:32] = tiles(3 * p + 2, 4 * p + 3)
        return carry

    lax.fori_loop(0, 64, pack, 0)
    LAND[me] = X[8 * gi + di]
    loads[2].wait()
    pl.semaphore_wait(barrier, 127)

    net = Copies(send_sem, recv_sem)
    rows = pl.ds(pl.multiple_of(c * 16, 16), 16)
    columns = pl.ds(pl.multiple_of(x * 384, 128), 384)
    latents = [
        net.send(QLS.at[0, rows, columns], QLS.at[8 - j, rows, columns], (di + j) % 8, "dp")
        for j in range(1, 8)
    ]

    def deal(j, carry):
        dd, gg = there(j)
        pltpu.make_async_remote_copy(
            src_ref=X.at[8 * gg + dd],
            dst_ref=LAND.at[me],
            send_sem=all_send,
            recv_sem=all_recv,
            device_id={"dp": dd, "grp": gg},
            device_id_type=MESH,
        ).start()
        return carry

    lax.fori_loop(1, 128, deal, 0)
    for copy in latents:
        copy.wait_recv()
    piece = QLS.at[1:8, rows, columns]
    latents = [net.send(piece, piece, p) for p in (p_xp, p_xm, p_x2)]

    to = lax.broadcasted_iota(jnp.int32, (256, 256), 0)
    was = lax.broadcasted_iota(jnp.int32, (256, 256), 1)
    within = jnp.where(to < 96, to, to - 96)
    twelve = jnp.where(to < 96, to, to - 80)
    for n in range(1, 8):
        twelve = twelve + jnp.where(within >= 12 * n, 20, 0)
    four = 32 * ((to % 32) // 4) + to % 4 + jnp.where(to < 224, 12, 28)
    half = to - to % 32 + ((to % 16) // 4) * 8 + ((to % 32) // 16) * 4 + to % 4
    MOVE[0] = (was == jnp.where(to < 192, twelve, four)).astype(f32).astype(bf)
    MOVE[1] = (was == half).astype(f32).astype(bf)
    MOVE[2] = (was == ((to // 4) % 8) * 16 + (to % 4) * 4 + to // 32).astype(f32).astype(bf)
    MOVE[3] = (was == (to % 8) * 32 + to // 8).astype(f32).astype(bf)
    SC[...] = jnp.zeros_like(SC)

    row = lax.broadcasted_iota(jnp.int32, (16, 128), 0)
    sign = jnp.where(lax.broadcasted_iota(jnp.int32, (16, 128), 1) % 2 == 0, -1.0, 1.0)
    turns = []
    for h in range(2):
        position = row // 4
        for r in range(4):
            position = position + jnp.where(row % 4 == r, len_ref[4 * h + r], 0)
        angle = position.astype(f32) * freq_ref[...]
        turns.append((jnp.cos(angle), sign * jnp.sin(angle)))

    for copy in latents:
        copy.wait_recv()
    net.send(QLS.at[1:8, rows], QLS.at[1:8, rows], p_c).wait_recv()
    pltpu.make_async_copy(LAND.at[0:127], LAND.at[0:127], all_recv).wait()

    for b in range(16):
        block = jnp.dot(
            MOVE[0], LAND[8 * b : 8 * b + 8].reshape(256, 128), preferred_element_type=f32
        ).astype(bf)
        W[0, 96 * b : 96 * b + 96] = block[0:96]
        W[1, 96 * b : 96 * b + 96] = block[96:192]
        KC[32 * b : 32 * b + 32] = block[192:224]
        WV[di, 32 * b : 32 * b + 32] = block[224:256]
    latent_in = QLS[...].reshape(256, QL)
    qa = jnp.dot(latent_in, W[0], preferred_element_type=f32).astype(bf)
    qb = jnp.dot(latent_in, W[1], preferred_element_type=f32).astype(bf)
    qa = jnp.dot(MOVE[1], qa, preferred_element_type=f32)
    qb = jnp.dot(MOVE[1], qb, preferred_element_type=f32)
    ra, rb = pltpu.roll(qa, 64, 1), pltpu.roll(qb, 64, 1)
    lane = lax.broadcasted_iota(jnp.int32, (256, 128), 1)
    odd = di % 2 == 1
    plain = jnp.where(odd, jnp.where(lane < 64, ra, rb), qa).astype(bf)
    rotary = jnp.where(lane < 64, jnp.where(odd, rb, qb), 0.0).astype(bf)
    absorbed = lax.dot_general(plain, KC[...], nt, preferred_element_type=f32).astype(bf)
    E[:, :, 0:KVL] = absorbed.reshape(8, 32, KVL)
    E[:, :, KVL:WIDE] = rotary.reshape(8, 32, 128)
    heads = []
    for h in range(2):
        span = pl.ds(16 * h, 16)
        heads.append(
            [net.send(E.at[j, span], QR.at[h, di], (di + j) % 8, "dp") for j in range(1, 8)]
        )
        QR[h, di] = E[0, span]
    loads[3].wait()
    to_log2 = float(NOPE + ROPE) ** -0.5 * LOG2E

    def place(h):
        for copy in heads[h]:
            copy.wait_recv()
        span = pl.ds(4 * h, 4)
        rotary = QR[h, :, :, KVL:WIDE].reshape(128, 128).astype(f32)
        even = lax.broadcasted_iota(jnp.int32, (128, 128), 1) % 2 == 0
        other = jnp.where(even, pltpu.roll(rotary, 127, 1), pltpu.roll(rotary, 1, 1))
        cosine, sine = turns[h]
        rotary = rotary.reshape(8, 16, 128) * cosine[None] + other.reshape(8, 16, 128) * sine[None]
        move = MOVE[2, 0:128, 0:128]
        absorbed = jnp.dot(move, QR[h, :, :, 0:KVL].reshape(128, KVL), preferred_element_type=f32)
        rotary = jnp.dot(move, rotary.reshape(128, 128).astype(bf), preferred_element_type=f32)
        G[span, pl.ds(gi, 1), :, 0:KVL] = absorbed.astype(bf).reshape(4, 1, 32, KVL)
        G[span, pl.ds(gi, 1), :, KVL:WIDTH] = rotary[:, :ROPE].astype(bf).reshape(4, 1, 32, ROPE)

    def new_scores(h):
        query = lax.broadcasted_iota(jnp.int32, (128, 32), 0)
        key = lax.broadcasted_iota(jnp.int32, (128, 32), 1)
        live = (key % 8 == 4 * h + query // 32) & (key // 8 <= query % 4)
        score = lax.dot_general(
            G[pl.ds(4 * h, 4), pl.ds(gi, 1)].reshape(128, WIDTH), NEW[...], nt,
            preferred_element_type=f32,
        )
        SN[pl.ds(128 * h, 128)] = jnp.where(live, score * to_log2, -1e30)

    def gather(h):
        b = 4 * h
        A, B = (b, 2), (b + 2, 2)
        s_l, s_r, s_z = p_xm, p_xp, p_z
        s_lz, s_rz, s_f, s_fz = at(xm, zo, c), at(xp, zo, c), p_x2, at(x2, zo, c)

        def go(span, slot, peer):
            block = G.at[pl.ds(span[0], span[1]), slot]
            return net.send(block, block, peer)

        mate = []

        def share(span, slot):
            mate.append(go(span, slot, p_c))

        z_a = go(A, gi, p_z)
        l_b, r_b = go(B, gi, p_xp), go(B, gi, p_xm)
        l_a, r_a = go(A, gi, p_xp), go(A, gi, p_xm)
        share((b, 4), gi)
        z_b = go(B, gi, p_z)
        yield
        z_a.wait_recv()
        lz_a, rz_a = go(A, s_z, p_xp), go(A, s_z, p_xm)
        share(A, s_z)
        l_b.wait_recv()
        f0_b, lz_b = go((b + 2, 1), s_l, p_xp), go(B, s_l, p_z)
        share(B, s_l)
        r_b.wait_recv()
        f1_b, rz_b = go((b + 3, 1), s_r, p_xm), go(B, s_r, p_z)
        share(B, s_r)
        l_a.wait_recv()
        f0_a = go((b, 1), s_l, p_xp)
        share(A, s_l)
        r_a.wait_recv()
        f1_a = go((b + 1, 1), s_r, p_xm)
        share(A, s_r)
        yield
        lz_a.wait_recv()
        fz0_a = go((b, 1), s_lz, p_xp)
        share(A, s_lz)
        rz_a.wait_recv()
        fz1_a = go((b + 1, 1), s_rz, p_xm)
        share(A, s_rz)
        f0_b.wait_recv()
        fz0_b = go((b + 2, 1), s_f, p_z)
        f1_b.wait_recv()
        fz1_b = go((b + 3, 1), s_f, p_z)
        share(B, s_f)
        f0_a.wait_recv()
        f1_a.wait_recv()
        share(A, s_f)
        yield
        z_b.wait_recv()
        share(B, s_z)
        lz_b.wait_recv()
        share(B, s_lz)
        rz_b.wait_recv()
        share(B, s_rz)
        fz0_a.wait_recv()
        fz1_a.wait_recv()
        share(A, s_fz)
        fz0_b.wait_recv()
        fz1_b.wait_recv()
        share(B, s_fz)
        yield
        for copy in mate:
            copy.wait_recv()
        yield

    lanes = lax.broadcasted_iota(jnp.int32, (512, 128), 1)
    key_at = lax.broadcasted_iota(jnp.int32, (1, 512), 1) + gi * 512
    own_rows = pl.ds(gi * 32, 32)

    def one_request(r, carry):
        h = r // 4
        q = G[r].reshape(512, WIDTH)
        k = K[r]
        s = jnp.dot(q, k, preferred_element_type=f32) * to_log2
        s = jnp.where(key_at < len_ref[r], s, -1e30)
        sn = SN[pl.ds(r * 32, 32), :]
        M[...] = jnp.broadcast_to(jnp.maximum(jnp.max(s, 1, keepdims=True), -1e29), (512, 128))
        M[own_rows, :] = jnp.maximum(M[own_rows, :], jnp.max(sn, 1, keepdims=True))
        p = jnp.exp2(s - M[:, 0:1])
        pn = jnp.exp2(sn - M[own_rows, 0:1])
        L[...] = jnp.broadcast_to(jnp.sum(p, 1, keepdims=True), (512, 128))
        L[own_rows, :] = L[own_rows, :] + jnp.sum(pn, 1, keepdims=True)
        O[r] = lax.dot_general(p.astype(bf), k[:KVL], nt, preferred_element_type=f32)
        O[r, own_rows, :] = O[r, own_rows, :] + jnp.dot(
            pn.astype(bf), NEW[:, :KVL], preferred_element_type=f32
        )
        both = jnp.transpose(jnp.where(lanes == 0, M[...], L[...]))
        ml_send[h, 0, pl.ds(r % 4, 1), :] = both[0:1]
        ml_send[h, 0, pl.ds(4 + r % 4, 1), :] = both[1:2]
        return carry

    def work(r):
        lax.fori_loop(r, r + 1, one_request, 0)

    def peaks(h):
        def pair(ref):
            return ref[0:4], ref[4:8]

        mine = pair(ml_send[h, 0])
        total = mine
        for stage, peer in ((0, p_c), (1, p_z)):
            copy = net.send(ml_send.at[h, stage], ml_recv.at[h, stage], peer)
            yield
            copy.wait_recv()
            total = merge(total, pair(ml_recv[h, stage]))
            ml_send[h, stage + 1, 0:4] = total[0]
            ml_send[h, stage + 1, 4:8] = total[1]
        last = [
            net.send(ml_send.at[h, 2], ml_recv.at[h, 2 + j], p)
            for j, p in enumerate((p_xp, p_xm, p_x2))
        ]
        yield
        for j, copy in enumerate(last):
            copy.wait_recv()
            total = merge(total, pair(ml_recv[h, 2 + j]))
        SC[0:4] = jnp.exp2(mine[0] - total[0]) / total[1]
        SCT[h] = jnp.transpose(SC[...])
        yield

    def add(*terms):
        total = terms[0].astype(f32)
        for term in terms[1:]:
            total = total + term.astype(f32)
        return total.astype(bf)

    def reduce(h):
        b = 4 * h
        two = pl.ds(b, 2), pl.ds(b + 2, 2)
        mate = []
        for n in range(2):
            for r in (b + 2 * n, b + 2 * n + 1):
                part = (O[r] * SCT[h, :, r - b : r - b + 1]).astype(bf)
                NB[r] = part.reshape(4, 2, 2, 32, KVL)
            mate.append(net.send(NB.at[two[n], :, :, co], RD.at[two[n]], p_c))
        yield
        mate[0].wait_recv()
        for r in (b, b + 1):
            T[r] = add(NB[r, :, :, c], RD[r])
        f0 = net.send(T.at[b, x2], RFA.at[h, 0], p_xp)
        f1 = net.send(T.at[b + 1, x2], RFA.at[h, 1], p_xm)
        l1 = net.send(T.at[b + 1, xp], RLA.at[h, 1], p_xp)
        r0 = net.send(T.at[b, xm], RRA.at[h, 0], p_xm)
        mate[1].wait_recv()
        for r in (b + 2, b + 3):
            T[r] = add(NB[r, :, :, c], RD[r])
        z_b = net.send(T.at[two[1], :, zo], RZB.at[h], p_z)
        yield
        f0.wait_recv()
        T[b, xp] = add(T[b, xp], RFA[h, 0])
        l0 = net.send(T.at[b, xp], RLA.at[h, 0], p_xp)
        f1.wait_recv()
        T[b + 1, xm] = add(T[b + 1, xm], RFA[h, 1])
        r1 = net.send(T.at[b + 1, xm], RRA.at[h, 1], p_xm)
        z_b.wait_recv()
        for n in range(2):
            V[h, n] = add(T[b + 2 + n, :, zl], RZB[h, n])
        g0 = net.send(V.at[h, 0, x2], RFB.at[h, 0], p_xp)
        g1 = net.send(V.at[h, 1, x2], RFB.at[h, 1], p_xm)
        k1 = net.send(V.at[h, 1, xp], RLB.at[h, 1], p_xp)
        q0 = net.send(V.at[h, 0, xm], RRB.at[h, 0], p_xm)
        yield
        for copy in (l1, r0, l0, r1):
            copy.wait_recv()
        for n in range(2):
            U[h, n] = add(T[b + n, x], RLA[h, n], RRA[h, n])
        z_a = net.send(U.at[h, :, zo], RZA.at[h], p_z)
        g0.wait_recv()
        V[h, 0, xp] = add(V[h, 0, xp], RFB[h, 0])
        k0 = net.send(V.at[h, 0, xp], RLB.at[h, 0], p_xp)
        g1.wait_recv()
        V[h, 1, xm] = add(V[h, 1, xm], RFB[h, 1])
        q1 = net.send(V.at[h, 1, xm], RRB.at[h, 1], p_xm)
        yield
        z_a.wait_recv()
        F[two[0]] = add(U[h, :, zl], RZA[h])
        for copy in (k1, q0, k0, q1):
            copy.wait_recv()
        F[two[1]] = add(V[h, :, x], RLB[h], RRB[h])
        yield

    def values():
        partner = (di + 4) % 8
        around = [(di // 4) * 4 + (di + j) % 4 for j in range(1, 4)]
        mine = [net.send(WV.at[di], WV.at[di], p, "dp") for p in around]
        yield
        over = net.send(WV.at[di], WV.at[di], partner, "dp")
        yield
        over.wait_recv()
        mine += [net.send(WV.at[partner], WV.at[partner], p, "dp") for p in around]
        yield
        for copy in mine:
            copy.wait_recv()
        yield

    gather0, gather1 = gather(0), gather(1)
    peaks0, peaks1 = peaks(0), peaks(1)
    reduce0, reduce1 = reduce(0), reduce(1)
    weights = values()
    place(0)
    next(gather0)
    place(1)
    new_scores(0)
    new_scores(1)
    next(weights)
    next(gather0)
    next(gather0)
    next(gather1)
    next(weights)
    next(gather0)
    loads[4].wait()
    next(gather0)
    work(0)
    next(gather1)
    work(1)
    next(gather1)
    work(2)
    next(gather1)
    work(3)
    next(peaks0)
    next(weights)
    next(gather1)
    next(peaks0)
    work(4)
    next(peaks0)
    work(5)
    next(peaks0)
    next(reduce0)
    work(6)
    next(reduce0)
    work(7)
    next(peaks1)
    next(reduce0)
    next(peaks1)
    next(peaks1)
    next(reduce0)
    next(peaks1)
    next(reduce1)
    next(reduce0)
    next(reduce1)
    next(reduce1)
    next(reduce1)
    next(weights)
    next(reduce1)

    latent = jnp.dot(MOVE[3], F[...].reshape(256, KVL), preferred_element_type=f32).astype(bf)
    for i in range(8):
        out_ref[:, i * VDIM : (i + 1) * VDIM] = jnp.dot(
            latent[i * 32 : (i + 1) * 32], WV[i], preferred_element_type=f32
        ).astype(bf)
    net.finish()
    pltpu.make_async_copy(X.at[0:127], X.at[0:127], all_send).wait()


def per_device(query_latent, q_up, kv_up, latent_cache, new_latent, lengths):
    bf, f32 = jnp.bfloat16, jnp.float32
    pair = np.arange(128) // 2
    freq = np.where(pair < ROPE // 2, 10000.0 ** (-(2.0 * pair) / ROPE), 0.0).astype(np.float32)
    vmem = pl.BlockSpec(memory_space=pltpu.VMEM)
    copies = 160
    out = pl.pallas_call(
        kernel,
        out_shape=jax.ShapeDtypeStruct((32, 8 * VDIM), bf),
        in_specs=[pl.BlockSpec(memory_space=pltpu.SMEM), vmem] + [pl.BlockSpec(memory_space=pl.ANY)] * 5,
        out_specs=vmem,
        scratch_shapes=[
            pltpu.VMEM((12, H * (NOPE + ROPE)), bf),
            pltpu.VMEM((4, H * (NOPE + VDIM)), bf),
            pltpu.VMEM((32, WIDTH), bf),
            pltpu.VMEM((4, 256, 256), bf),
            pltpu.VMEM((256, 32), f32),
            pltpu.VMEM((128, 32, 128), bf),
            pltpu.VMEM((128, 32, 128), bf),
            pltpu.VMEM((8, 32, QL), bf),
            pltpu.VMEM((2, QL, 128), bf),
            pltpu.VMEM((KVL, NOPE), bf),
            pltpu.VMEM((8, 32, WIDE), bf),
            pltpu.VMEM((2, 8, 16, WIDE), bf),
            pltpu.VMEM((8, KVL, VDIM), bf),
            pltpu.VMEM((8, 16, 32, WIDTH), bf),
            pltpu.VMEM((8, WIDTH, 512), bf),
            pltpu.VMEM((8, 512, KVL), f32),
            pltpu.VMEM((8, 4, 2, 2, 32, KVL), bf),
            pltpu.VMEM((8, 4, 2, 32, KVL), bf),
            pltpu.VMEM((8, 4, 2, 32, KVL), bf),
            pltpu.VMEM((2, 2, 4, 32, KVL), bf),
            pltpu.VMEM((2, 2, 2, 32, KVL), bf),
            pltpu.VMEM((2, 2, 2, 32, KVL), bf),
            pltpu.VMEM((2, 2, 2, 32, KVL), bf),
            pltpu.VMEM((2, 2, 2, 32, KVL), bf),
            pltpu.VMEM((2, 2, 32, KVL), bf),
            pltpu.VMEM((2, 2, 32, KVL), bf),
            pltpu.VMEM((2, 2, 32, KVL), bf),
            pltpu.VMEM((2, 2, 32, KVL), bf),
            pltpu.VMEM((2, 2, 4, 32, KVL), bf),
            pltpu.VMEM((512, 128), f32),
            pltpu.VMEM((512, 128), f32),
            pltpu.VMEM((2, 3, 8, 512), f32),
            pltpu.VMEM((2, 5, 8, 512), f32),
            pltpu.VMEM((128, 512), f32),
            pltpu.VMEM((2, 512, 128), f32),
            pltpu.VMEM((8, 32, KVL), bf),
            pltpu.SemaphoreType.DMA((copies,)),
            pltpu.SemaphoreType.DMA((copies,)),
            pltpu.SemaphoreType.DMA((5,)),
            pltpu.SemaphoreType.DMA,
            pltpu.SemaphoreType.DMA,
        ],
        compiler_params=pltpu.CompilerParams(
            collective_id=1, has_side_effects=True, vmem_limit_bytes=60 * 1024 * 1024
        ),
    )(
        lengths, jnp.asarray(freq)[None], query_latent.reshape(32, QL), q_up, kv_up,
        latent_cache.transpose(0, 2, 1), new_latent.reshape(32, WIDTH),
    )
    return out.reshape(STEPS, 8, 8 * VDIM)


def solution(mesh):
    return jax.shard_map(
        per_device,
        mesh=mesh,
        in_specs=(
            P(None, "dp", None),
            P(("dp", "grp"), None),
            P(("dp", "grp"), None),
            P("dp", "grp", None),
            P(None, "dp", None),
            P("dp"),
        ),
        out_specs=P(None, "dp", "grp"),
        check_vma=False,
    )
```

time: 116 us -> 108 us (0.931)
  Pallas kernels: 113 us -> 105 us
    pallas_call x1, Pallas kernels: 113 us -> 105 us  [per_device(): pl.pallas_call(kernel, out_shape=jax.ShapeDtypeStruct((32, 8 * VDIM), bf)...]
where the time goes in v4:
time: 108 us; the launch traced here: 107 us
  Pallas kernels  105 us (97%)
  local copies, waits for them, and re-layouts  1.47 us (1%)
    pallas_call x1, Pallas kernels, per_device(): pl.pallas_call(kernel, out_shape=jax.ShapeDtypeStruct((32, 8 * VDIM), bf)...  105 us

profile of v4, /device:TPU:0, one launch (start us, length us, event | category | flops | bytes accessed | tf_op | source)
XLA Modules:
  0.0 106.9 jit_solution(5115378431632063781)
XLA Ops:
  0.0 105.4 %shard_map.73 = bf16[32,1024]{1,0:T(8,128)(2,1)} custom-call(s32[8]{0:T(128)} %len_ref.1, f32[1,128]{1,0:T(1,128)} %constant.5.freq_ref, bf16[32,1536]{1,0:T(8,128)(2,1)} %bitcast.6, bf16[12,24576]{1,0:T(8,128)(2,1)} %q_ref.1, bf16[4,32768]{1,0:T(4,128)(2,1)} %kv_ref.1, bf16[8,576,512]{2,1,0:T(8,128)(2,1)} %bitcast.4, bf16[32,576]{1,0:T(8,128)(2,1)} %bitcast.7), custom_call_target="tpu_custom_call" | custom-call | tf_op jit(solution)/shard_map/pallas_call | solution.py:488
  105.4 1.5 %copy.9 = bf16[4,8,1024]{2,1,0:T(8,128)(2,1)} copy(bf16[4,8,1024]{2,1,0:T(8,128)(2,1)} %bitcast.5) | data formatting | bytes 131072

commit v5 on v4

--- a/solution.py
+++ b/solution.py
@@ -18,19 +18,29 @@
 WIDTH = KVL + ROPE
 WIDE = KVL + 128
 LOG2E = 1.4426950408889634
+POOL = 40
+GROUPS = 68
+SPLIT = 40
 
 
 class Copies:
     def __init__(self, send_sem, recv_sem):
-        self.send_sem, self.recv_sem, self.sent = send_sem, recv_sem, []
-
-    def send(self, src, dst, peer, axis="grp"):
+        self.send_sem, self.recv_sem, self.sent, self.groups = send_sem, recv_sem, [], 0
+
+    def group(self):
+        self.groups += 1
+        assert self.groups <= GROUPS
+        return self.groups - 1
+
+    def send(self, src, dst, peer, axis="grp", group=None):
         k = len(self.sent)
+        if k >= POOL:
+            self.sent[k - POOL].wait_send()
         copy = pltpu.make_async_remote_copy(
             src_ref=src,
             dst_ref=dst,
-            send_sem=self.send_sem.at[k],
-            recv_sem=self.recv_sem.at[k],
+            send_sem=self.send_sem.at[k % POOL],
+            recv_sem=self.recv_sem.at[self.group() if group is None else group],
             device_id={axis: peer},
             device_id_type=MESH,
         )
@@ -38,20 +48,18 @@
         self.sent.append(copy)
         return copy
 
+    def arrive(self, group, like):
+        pltpu.make_async_copy(like, like, self.recv_sem.at[group]).wait()
+
     def finish(self):
-        for copy in self.sent:
+        for copy in self.sent[-POOL:]:
             copy.wait_send()
-
-
-def merge(a, b):
-    peak = jnp.maximum(a[0], b[0])
-    return peak, a[1] * jnp.exp2(a[0] - peak) + b[1] * jnp.exp2(b[0] - peak)
 
 
 def kernel(
     len_ref, freq_ref, ql_ref, q_ref, kv_ref, cache_ref, new_ref, out_ref,
     QIN, KVIN, NEW, MOVE, SN, X, LAND, QLS, W, KC, E, QR, WV,
-    G, K, O, NB, RD, T, V, U, RFA, RLA, RRA, RZA, RFB, RLB, RRB, RZB, M, L, ml_send, ml_recv, SC, SCT, F,
+    G, K, O, NB, RD, T, V, U, RFA, RLA, RRA, RZA, RFB, RLB, RRB, RZB, S, M, L, sums, ml_send, ml_recv, SC, SCT, F,
     send_sem, recv_sem, load_sem, all_send, all_recv,
 ):
     di, gi = lax.axis_index("dp"), lax.axis_index("grp")
@@ -114,10 +122,10 @@
     net = Copies(send_sem, recv_sem)
     rows = pl.ds(pl.multiple_of(c * 16, 16), 16)
     columns = pl.ds(pl.multiple_of(x * 384, 128), 384)
-    latents = [
-        net.send(QLS.at[0, rows, columns], QLS.at[8 - j, rows, columns], (di + j) % 8, "dp")
-        for j in range(1, 8)
-    ]
+    piece = QLS.at[1:8, rows, columns]
+    first, second = net.group(), net.group()
+    for j in range(1, 8):
+        net.send(QLS.at[0, rows, columns], QLS.at[8 - j, rows, columns], (di + j) % 8, "dp", first)
 
     def deal(j, carry):
         dd, gg = there(j)
@@ -131,11 +139,11 @@
         ).start()
         return carry
 
-    lax.fori_loop(1, 128, deal, 0)
-    for copy in latents:
-        copy.wait_recv()
-    piece = QLS.at[1:8, rows, columns]
-    latents = [net.send(piece, piece, p) for p in (p_xp, p_xm, p_x2)]
+    lax.fori_loop(1, SPLIT, deal, 0)
+    net.arrive(first, piece)
+    for p in (p_xp, p_xm, p_x2):
+        net.send(piece, piece, p, group=second)
+    lax.fori_loop(SPLIT, 128, deal, 0)
 
     to = lax.broadcasted_iota(jnp.int32, (256, 256), 0)
     was = lax.broadcasted_iota(jnp.int32, (256, 256), 1)
@@ -150,6 +158,7 @@
     MOVE[2] = (was == ((to // 4) % 8) * 16 + (to % 4) * 4 + to // 32).astype(f32).astype(bf)
     MOVE[3] = (was == (to % 8) * 32 + to // 8).astype(f32).astype(bf)
     SC[...] = jnp.zeros_like(SC)
+    ml_send[...] = jnp.zeros_like(ml_send)
 
     row = lax.broadcasted_iota(jnp.int32, (16, 128), 0)
     sign = jnp.where(lax.broadcasted_iota(jnp.int32, (16, 128), 1) % 2 == 0, -1.0, 1.0)
@@ -161,8 +170,7 @@
         angle = position.astype(f32) * freq_ref[...]
         turns.append((jnp.cos(angle), sign * jnp.sin(angle)))
 
-    for copy in latents:
-        copy.wait_recv()
+    net.arrive(second, QLS.at[1:8, rows, 0:1152])
     net.send(QLS.at[1:8, rows], QLS.at[1:8, rows], p_c).wait_recv()
     pltpu.make_async_copy(LAND.at[0:127], LAND.at[0:127], all_recv).wait()
 
@@ -190,16 +198,15 @@
     heads = []
     for h in range(2):
         span = pl.ds(16 * h, 16)
-        heads.append(
-            [net.send(E.at[j, span], QR.at[h, di], (di + j) % 8, "dp") for j in range(1, 8)]
-        )
+        heads.append(net.group())
+        for j in range(1, 8):
+            net.send(E.at[j, span], QR.at[h, di], (di + j) % 8, "dp", heads[h])
         QR[h, di] = E[0, span]
     loads[3].wait()
     to_log2 = float(NOPE + ROPE) ** -0.5 * LOG2E
 
     def place(h):
-        for copy in heads[h]:
-            copy.wait_recv()
+        net.arrive(heads[h], QR.at[h, 0:7])
         span = pl.ds(4 * h, 4)
         rotary = QR[h, :, :, KVL:WIDE].reshape(128, 128).astype(f32)
         even = lax.broadcasted_iota(jnp.int32, (128, 128), 1) % 2 == 0
@@ -228,14 +235,14 @@
         s_l, s_r, s_z = p_xm, p_xp, p_z
         s_lz, s_rz, s_f, s_fz = at(xm, zo, c), at(xp, zo, c), p_x2, at(x2, zo, c)
 
-        def go(span, slot, peer):
+        def go(span, slot, peer, group=None):
             block = G.at[pl.ds(span[0], span[1]), slot]
-            return net.send(block, block, peer)
-
-        mate = []
+            return net.send(block, block, peer, group=group)
+
+        mate, far, far_a, far_b = net.group(), net.group(), net.group(), net.group()
 
         def share(span, slot):
-            mate.append(go(span, slot, p_c))
+            go(span, slot, p_c, mate)
 
         z_a = go(A, gi, p_z)
         l_b, r_b = go(B, gi, p_xp), go(B, gi, p_xm)
@@ -253,25 +260,24 @@
         f1_b, rz_b = go((b + 3, 1), s_r, p_xm), go(B, s_r, p_z)
         share(B, s_r)
         l_a.wait_recv()
-        f0_a = go((b, 1), s_l, p_xp)
+        go((b, 1), s_l, p_xp, far)
         share(A, s_l)
         r_a.wait_recv()
-        f1_a = go((b + 1, 1), s_r, p_xm)
+        go((b + 1, 1), s_r, p_xm, far)
         share(A, s_r)
         yield
         lz_a.wait_recv()
-        fz0_a = go((b, 1), s_lz, p_xp)
+        go((b, 1), s_lz, p_xp, far_a)
         share(A, s_lz)
         rz_a.wait_recv()
-        fz1_a = go((b + 1, 1), s_rz, p_xm)
+        go((b + 1, 1), s_rz, p_xm, far_a)
         share(A, s_rz)
         f0_b.wait_recv()
-        fz0_b = go((b + 2, 1), s_f, p_z)
+        go((b + 2, 1), s_f, p_z, far_b)
         f1_b.wait_recv()
-        fz1_b = go((b + 3, 1), s_f, p_z)
+        go((b + 3, 1), s_f, p_z, far_b)
         share(B, s_f)
-        f0_a.wait_recv()
-        f1_a.wait_recv()
+        net.arrive(far, G.at[pl.ds(b, 2), 0])
         share(A, s_f)
         yield
         z_b.wait_recv()
@@ -280,76 +286,88 @@
         share(B, s_lz)
         rz_b.wait_recv()
         share(B, s_rz)
-        fz0_a.wait_recv()
-        fz1_a.wait_recv()
+        net.arrive(far_a, G.at[pl.ds(b, 2), 0])
         share(A, s_fz)
-        fz0_b.wait_recv()
-        fz1_b.wait_recv()
+        net.arrive(far_b, G.at[pl.ds(b, 2), 0])
         share(B, s_fz)
         yield
-        for copy in mate:
-            copy.wait_recv()
+        net.arrive(mate, G.at[pl.ds(b, 4), 0:8])
         yield
 
     lanes = lax.broadcasted_iota(jnp.int32, (512, 128), 1)
     key_at = lax.broadcasted_iota(jnp.int32, (1, 512), 1) + gi * 512
     own_rows = pl.ds(gi * 32, 32)
 
-    def one_request(r, carry):
-        h = r // 4
-        q = G[r].reshape(512, WIDTH)
-        k = K[r]
-        s = jnp.dot(q, k, preferred_element_type=f32) * to_log2
+    def score_one(r, carry):
+        s = jnp.dot(G[r].reshape(512, WIDTH), K[r], preferred_element_type=f32) * to_log2
         s = jnp.where(key_at < len_ref[r], s, -1e30)
-        sn = SN[pl.ds(r * 32, 32), :]
-        M[...] = jnp.broadcast_to(jnp.maximum(jnp.max(s, 1, keepdims=True), -1e29), (512, 128))
-        M[own_rows, :] = jnp.maximum(M[own_rows, :], jnp.max(sn, 1, keepdims=True))
-        p = jnp.exp2(s - M[:, 0:1])
-        pn = jnp.exp2(sn - M[own_rows, 0:1])
+        S[r % 4] = s
+        peak = jnp.maximum(jnp.max(s, 1, keepdims=True), -1e29)
+        M[r] = jnp.broadcast_to(peak, (512, 128))
+        M[r, own_rows, :] = jnp.maximum(
+            M[r, own_rows, :], jnp.max(SN[pl.ds(r * 32, 32), :], 1, keepdims=True)
+        )
+        ml_send[r // 4, 0, pl.ds(r % 4, 1), :] = jnp.transpose(M[r])[0:1]
+        return carry
+
+    def value_one(r, carry):
+        p = jnp.exp2(S[r % 4] - M[r, :, 0:1])
+        pn = jnp.exp2(SN[pl.ds(r * 32, 32), :] - M[r, own_rows, 0:1])
         L[...] = jnp.broadcast_to(jnp.sum(p, 1, keepdims=True), (512, 128))
         L[own_rows, :] = L[own_rows, :] + jnp.sum(pn, 1, keepdims=True)
-        O[r] = lax.dot_general(p.astype(bf), k[:KVL], nt, preferred_element_type=f32)
+        O[r] = lax.dot_general(p.astype(bf), K[r, 0:KVL], nt, preferred_element_type=f32)
         O[r, own_rows, :] = O[r, own_rows, :] + jnp.dot(
             pn.astype(bf), NEW[:, :KVL], preferred_element_type=f32
         )
-        both = jnp.transpose(jnp.where(lanes == 0, M[...], L[...]))
-        ml_send[h, 0, pl.ds(r % 4, 1), :] = both[0:1]
-        ml_send[h, 0, pl.ds(4 + r % 4, 1), :] = both[1:2]
+        sums[pl.ds(r, 1), :] = jnp.transpose(L[...])[0:1]
         return carry
 
-    def work(r):
-        lax.fori_loop(r, r + 1, one_request, 0)
-
-    def peaks(h):
-        def pair(ref):
-            return ref[0:4], ref[4:8]
-
-        mine = pair(ml_send[h, 0])
-        total = mine
+    def score(first, count):
+        lax.fori_loop(first, first + count, score_one, 0)
+
+    def value(first, count):
+        lax.fori_loop(first, first + count, value_one, 0)
+
+    def butterfly(n, join):
+        total = ml_send[n, 0]
         for stage, peer in ((0, p_c), (1, p_z)):
-            copy = net.send(ml_send.at[h, stage], ml_recv.at[h, stage], peer)
+            copy = net.send(ml_send.at[n, stage], ml_recv.at[n, stage], peer)
             yield
             copy.wait_recv()
-            total = merge(total, pair(ml_recv[h, stage]))
-            ml_send[h, stage + 1, 0:4] = total[0]
-            ml_send[h, stage + 1, 4:8] = total[1]
-        last = [
-            net.send(ml_send.at[h, 2], ml_recv.at[h, 2 + j], p)
-            for j, p in enumerate((p_xp, p_xm, p_x2))
-        ]
-        yield
-        for j, copy in enumerate(last):
-            copy.wait_recv()
-            total = merge(total, pair(ml_recv[h, 2 + j]))
-        SC[0:4] = jnp.exp2(mine[0] - total[0]) / total[1]
+            total = join(total, ml_recv[n, stage])
+            ml_send[n, stage + 1] = total
+        last = net.group()
+        for j, p in enumerate((p_xp, p_xm, p_x2)):
+            net.send(ml_send.at[n, 2], ml_recv.at[n, 2 + j], p, group=last)
+        yield
+        net.arrive(last, ml_recv.at[n, 2:5])
+        for j in range(3):
+            total = join(total, ml_recv[n, 2 + j])
+        ml_send[n, 3] = total
+
+    def peaks(h):
+        yield from butterfly(h, jnp.maximum)
+        factor = jnp.exp2(ml_send[h, 0] - ml_send[h, 3])
+        sums[4 * h : 4 * h + 4] = sums[4 * h : 4 * h + 4] * factor[0:4]
+        SC[0:8] = factor
         SCT[h] = jnp.transpose(SC[...])
         yield
 
-    def add(*terms):
+    def totals():
+        ml_send[2, 0] = sums[...]
+        yield from butterfly(2, jnp.add)
+        SC[0:8] = ml_send[2, 3]
+        SCT[2] = jnp.transpose(SC[...])
+        yield
+
+    def total_of(*terms):
         total = terms[0].astype(f32)
         for term in terms[1:]:
             total = total + term.astype(f32)
-        return total.astype(bf)
+        return total
+
+    def add(*terms):
+        return total_of(*terms).astype(bf)
 
     def reduce(h):
         b = 4 * h
@@ -366,8 +384,9 @@
             T[r] = add(NB[r, :, :, c], RD[r])
         f0 = net.send(T.at[b, x2], RFA.at[h, 0], p_xp)
         f1 = net.send(T.at[b + 1, x2], RFA.at[h, 1], p_xm)
-        l1 = net.send(T.at[b + 1, xp], RLA.at[h, 1], p_xp)
-        r0 = net.send(T.at[b, xm], RRA.at[h, 0], p_xm)
+        near_a, near_b = net.group(), net.group()
+        net.send(T.at[b + 1, xp], RLA.at[h, 1], p_xp, group=near_a)
+        net.send(T.at[b, xm], RRA.at[h, 0], p_xm, group=near_a)
         mate[1].wait_recv()
         for r in (b + 2, b + 3):
             T[r] = add(NB[r, :, :, c], RD[r])
@@ -375,55 +394,55 @@
         yield
         f0.wait_recv()
         T[b, xp] = add(T[b, xp], RFA[h, 0])
-        l0 = net.send(T.at[b, xp], RLA.at[h, 0], p_xp)
+        net.send(T.at[b, xp], RLA.at[h, 0], p_xp, group=near_a)
         f1.wait_recv()
         T[b + 1, xm] = add(T[b + 1, xm], RFA[h, 1])
-        r1 = net.send(T.at[b + 1, xm], RRA.at[h, 1], p_xm)
+        net.send(T.at[b + 1, xm], RRA.at[h, 1], p_xm, group=near_a)
         z_b.wait_recv()
         for n in range(2):
             V[h, n] = add(T[b + 2 + n, :, zl], RZB[h, n])
         g0 = net.send(V.at[h, 0, x2], RFB.at[h, 0], p_xp)
         g1 = net.send(V.at[h, 1, x2], RFB.at[h, 1], p_xm)
-        k1 = net.send(V.at[h, 1, xp], RLB.at[h, 1], p_xp)
-        q0 = net.send(V.at[h, 0, xm], RRB.at[h, 0], p_xm)
-        yield
-        for copy in (l1, r0, l0, r1):
-            copy.wait_recv()
+        net.send(V.at[h, 1, xp], RLB.at[h, 1], p_xp, group=near_b)
+        net.send(V.at[h, 0, xm], RRB.at[h, 0], p_xm, group=near_b)
+        yield
+        net.arrive(near_a, RLA)
         for n in range(2):
             U[h, n] = add(T[b + n, x], RLA[h, n], RRA[h, n])
         z_a = net.send(U.at[h, :, zo], RZA.at[h], p_z)
         g0.wait_recv()
         V[h, 0, xp] = add(V[h, 0, xp], RFB[h, 0])
-        k0 = net.send(V.at[h, 0, xp], RLB.at[h, 0], p_xp)
+        net.send(V.at[h, 0, xp], RLB.at[h, 0], p_xp, group=near_b)
         g1.wait_recv()
         V[h, 1, xm] = add(V[h, 1, xm], RFB[h, 1])
-        q1 = net.send(V.at[h, 1, xm], RRB.at[h, 1], p_xm)
+        net.send(V.at[h, 1, xm], RRB.at[h, 1], p_xm, group=near_b)
         yield
         z_a.wait_recv()
-        F[two[0]] = add(U[h, :, zl], RZA[h])
-        for copy in (k1, q0, k0, q1):
-            copy.wait_recv()
-        F[two[1]] = add(V[h, :, x], RLB[h], RRB[h])
+        F[two[0]] = total_of(U[h, :, zl], RZA[h])
+        net.arrive(near_b, RLB)
+        F[two[1]] = total_of(V[h, :, x], RLB[h], RRB[h])
         yield
 
     def values():
         partner = (di + 4) % 8
         around = [(di // 4) * 4 + (di + j) % 4 for j in range(1, 4)]
-        mine = [net.send(WV.at[di], WV.at[di], p, "dp") for p in around]
+        mine = net.group()
+        for p in around:
+            net.send(WV.at[di], WV.at[di], p, "dp", mine)
         yield
         over = net.send(WV.at[di], WV.at[di], partner, "dp")
         yield
         over.wait_recv()
-        mine += [net.send(WV.at[partner], WV.at[partner], p, "dp") for p in around]
-        yield
-        for copy in mine:
-            copy.wait_recv()
+        for p in around:
+            net.send(WV.at[partner], WV.at[partner], p, "dp", mine)
+        yield
+        net.arrive(mine, WV.at[0:6])
         yield
 
     gather0, gather1 = gather(0), gather(1)
     peaks0, peaks1 = peaks(0), peaks(1)
     reduce0, reduce1 = reduce(0), reduce(1)
-    weights = values()
+    weights, sum_up = values(), totals()
     place(0)
     next(gather0)
     place(1)
@@ -437,40 +456,48 @@
     next(gather0)
     loads[4].wait()
     next(gather0)
-    work(0)
+    score(0, 4)
+    next(peaks0)
     next(gather1)
-    work(1)
+    value(0, 2)
+    next(peaks0)
+    value(2, 2)
     next(gather1)
-    work(2)
-    next(gather1)
-    work(3)
     next(peaks0)
     next(weights)
     next(gather1)
     next(peaks0)
-    work(4)
-    next(peaks0)
-    work(5)
-    next(peaks0)
     next(reduce0)
-    work(6)
-    next(reduce0)
-    work(7)
+    next(gather1)
+    score(4, 4)
     next(peaks1)
     next(reduce0)
+    value(4, 1)
     next(peaks1)
+    value(5, 1)
     next(peaks1)
+    value(6, 1)
     next(reduce0)
+    value(7, 1)
     next(peaks1)
     next(reduce1)
+    next(sum_up)
+    next(reduce1)
+    next(sum_up)
     next(reduce0)
     next(reduce1)
+    next(sum_up)
+    next(reduce0)
     next(reduce1)
-    next(reduce1)
+    next(sum_up)
     next(weights)
     next(reduce1)
 
-    latent = jnp.dot(MOVE[3], F[...].reshape(256, KVL), preferred_element_type=f32).astype(bf)
+    for r in range(8):
+        F[r] = F[r] / SCT[2, own_rows, r : r + 1]
+    latent = jnp.dot(
+        MOVE[3], F[...].astype(bf).reshape(256, KVL), preferred_element_type=f32
+    ).astype(bf)
     for i in range(8):
         out_ref[:, i * VDIM : (i + 1) * VDIM] = jnp.dot(
             latent[i * 32 : (i + 1) * 32], WV[i], preferred_element_type=f32
@@ -484,7 +511,6 @@
     pair = np.arange(128) // 2
     freq = np.where(pair < ROPE // 2, 10000.0 ** (-(2.0 * pair) / ROPE), 0.0).astype(np.float32)
     vmem = pl.BlockSpec(memory_space=pltpu.VMEM)
-    copies = 160
     out = pl.pallas_call(
         kernel,
         out_shape=jax.ShapeDtypeStruct((32, 8 * VDIM), bf),
@@ -520,15 +546,17 @@
             pltpu.VMEM((2, 2, 32, KVL), bf),
             pltpu.VMEM((2, 2, 32, KVL), bf),
             pltpu.VMEM((2, 2, 4, 32, KVL), bf),
+            pltpu.VMEM((4, 512, 512), f32),
+            pltpu.VMEM((8, 512, 128), f32),
             pltpu.VMEM((512, 128), f32),
-            pltpu.VMEM((512, 128), f32),
-            pltpu.VMEM((2, 3, 8, 512), f32),
-            pltpu.VMEM((2, 5, 8, 512), f32),
+            pltpu.VMEM((8, 512), f32),
+            pltpu.VMEM((3, 4, 8, 512), f32),
+            pltpu.VMEM((3, 5, 8, 512), f32),
             pltpu.VMEM((128, 512), f32),
-            pltpu.VMEM((2, 512, 128), f32),
-            pltpu.VMEM((8, 32, KVL), bf),
-            pltpu.SemaphoreType.DMA((copies,)),
-            pltpu.SemaphoreType.DMA((copies,)),
+            pltpu.VMEM((3, 512, 128), f32),
+            pltpu.VMEM((8, 32, KVL), f32),
+            pltpu.SemaphoreType.DMA((POOL,)),
+            pltpu.SemaphoreType.DMA((GROUPS,)),
             pltpu.SemaphoreType.DMA((5,)),
             pltpu.SemaphoreType.DMA,
             pltpu.SemaphoreType.DMA,

time: 108 us -> 103 us (0.954)
  Pallas kernels: 105 us -> 100 us
    pallas_call x1, Pallas kernels: 105 us -> 100 us  [per_device(): pl.pallas_call(kernel, out_shape=jax.ShapeDtypeStruct((32, 8 * VDIM), bf)...]
where the time goes in v5:
time: 103 us; the launch traced here: 102 us
  Pallas kernels  100 us (97%)
  local copies, waits for them, and re-layouts  1.47 us (1%)
    pallas_call x1, Pallas kernels, per_device(): pl.pallas_call(kernel, out_shape=jax.ShapeDtypeStruct((32, 8 * VDIM), bf)...  100 us

profile of v5, /device:TPU:0, one launch (start us, length us, event | category | flops | bytes accessed | tf_op | source)
XLA Modules:
  0.0 101.7 jit_solution(11942951742342580749)
XLA Ops:
  0.0 100.2 %shard_map.73 = bf16[32,1024]{1,0:T(8,128)(2,1)} custom-call(s32[8]{0:T(128)} %len_ref.1, f32[1,128]{1,0:T(1,128)} %constant.5.freq_ref, bf16[32,1536]{1,0:T(8,128)(2,1)} %bitcast.6, bf16[12,24576]{1,0:T(8,128)(2,1)} %q_ref.1, bf16[4,32768]{1,0:T(4,128)(2,1)} %kv_ref.1, bf16[8,576,512]{2,1,0:T(8,128)(2,1)} %bitcast.4, bf16[32,576]{1,0:T(8,128)(2,1)} %bitcast.7), custom_call_target="tpu_custom_call" | custom-call | tf_op jit(solution)/shard_map/pallas_call | solution.py:514
  100.2 1.5 %copy.9 = bf16[4,8,1024]{2,1,0:T(8,128)(2,1)} copy(bf16[4,8,1024]{2,1,0:T(8,128)(2,1)} %bitcast.5) | data formatting | bytes 131072

commit v6 on v5

--- a/solution.py
+++ b/solution.py
@@ -19,8 +19,7 @@
 WIDE = KVL + 128
 LOG2E = 1.4426950408889634
 POOL = 40
-GROUPS = 68
-SPLIT = 40
+GROUPS = 73
 
 
 class Copies:
@@ -121,11 +120,9 @@
 
     net = Copies(send_sem, recv_sem)
     rows = pl.ds(pl.multiple_of(c * 16, 16), 16)
-    columns = pl.ds(pl.multiple_of(x * 384, 128), 384)
-    piece = QLS.at[1:8, rows, columns]
-    first, second = net.group(), net.group()
+    first = net.group()
     for j in range(1, 8):
-        net.send(QLS.at[0, rows, columns], QLS.at[8 - j, rows, columns], (di + j) % 8, "dp", first)
+        net.send(QLS.at[0, rows], QLS.at[8 - j, rows], (di + j) % 8, "dp", first)
 
     def deal(j, carry):
         dd, gg = there(j)
@@ -139,11 +136,7 @@
         ).start()
         return carry
 
-    lax.fori_loop(1, SPLIT, deal, 0)
-    net.arrive(first, piece)
-    for p in (p_xp, p_xm, p_x2):
-        net.send(piece, piece, p, group=second)
-    lax.fori_loop(SPLIT, 128, deal, 0)
+    lax.fori_loop(1, 128, deal, 0)
 
     to = lax.broadcasted_iota(jnp.int32, (256, 256), 0)
     was = lax.broadcasted_iota(jnp.int32, (256, 256), 1)
@@ -170,7 +163,7 @@
         angle = position.astype(f32) * freq_ref[...]
         turns.append((jnp.cos(angle), sign * jnp.sin(angle)))
 
-    net.arrive(second, QLS.at[1:8, rows, 0:1152])
+    net.arrive(first, QLS.at[1:8, rows])
     net.send(QLS.at[1:8, rows], QLS.at[1:8, rows], p_c).wait_recv()
     pltpu.make_async_copy(LAND.at[0:127], LAND.at[0:127], all_recv).wait()
 
@@ -371,45 +364,45 @@
 
     def reduce(h):
         b = 4 * h
-        two = pl.ds(b, 2), pl.ds(b + 2, 2)
-        mate = []
-        for n in range(2):
-            for r in (b + 2 * n, b + 2 * n + 1):
+        A, B = pl.ds(b, 2), pl.ds(b + 2, 2)
+        near_a, near_b = net.group(), net.group()
+        mate = {}
+        for first in (b + 2, b):
+            for r in (first, first + 1):
                 part = (O[r] * SCT[h, :, r - b : r - b + 1]).astype(bf)
                 NB[r] = part.reshape(4, 2, 2, 32, KVL)
-            mate.append(net.send(NB.at[two[n], :, :, co], RD.at[two[n]], p_c))
-        yield
-        mate[0].wait_recv()
+            span = pl.ds(first, 2)
+            mate[first] = net.send(NB.at[span, :, :, co], RD.at[span], p_c)
+        yield
+        mate[b + 2].wait_recv()
+        for r in (b + 2, b + 3):
+            T[r] = add(NB[r, :, :, c], RD[r])
+        over = [net.send(T.at[B, xx, zo], RZB.at[h, :, xx], p_z) for xx in (x2, xp, xm, x)]
+        mate[b].wait_recv()
         for r in (b, b + 1):
             T[r] = add(NB[r, :, :, c], RD[r])
         f0 = net.send(T.at[b, x2], RFA.at[h, 0], p_xp)
         f1 = net.send(T.at[b + 1, x2], RFA.at[h, 1], p_xm)
-        near_a, near_b = net.group(), net.group()
         net.send(T.at[b + 1, xp], RLA.at[h, 1], p_xp, group=near_a)
         net.send(T.at[b, xm], RRA.at[h, 0], p_xm, group=near_a)
-        mate[1].wait_recv()
-        for r in (b + 2, b + 3):
-            T[r] = add(NB[r, :, :, c], RD[r])
-        z_b = net.send(T.at[two[1], :, zo], RZB.at[h], p_z)
-        yield
+        yield
+        over[0].wait_recv()
+        V[h, :, x2] = add(T[B, x2, zl], RZB[h, :, x2])
+        g0 = net.send(V.at[h, 0, x2], RFB.at[h, 0], p_xp)
+        g1 = net.send(V.at[h, 1, x2], RFB.at[h, 1], p_xm)
         f0.wait_recv()
         T[b, xp] = add(T[b, xp], RFA[h, 0])
         net.send(T.at[b, xp], RLA.at[h, 0], p_xp, group=near_a)
         f1.wait_recv()
         T[b + 1, xm] = add(T[b + 1, xm], RFA[h, 1])
         net.send(T.at[b + 1, xm], RRA.at[h, 1], p_xm, group=near_a)
-        z_b.wait_recv()
-        for n in range(2):
-            V[h, n] = add(T[b + 2 + n, :, zl], RZB[h, n])
-        g0 = net.send(V.at[h, 0, x2], RFB.at[h, 0], p_xp)
-        g1 = net.send(V.at[h, 1, x2], RFB.at[h, 1], p_xm)
+        yield
+        over[1].wait_recv()
+        V[h, :, xp] = add(T[B, xp, zl], RZB[h, :, xp])
         net.send(V.at[h, 1, xp], RLB.at[h, 1], p_xp, group=near_b)
+        over[2].wait_recv()
+        V[h, :, xm] = add(T[B, xm, zl], RZB[h, :, xm])
         net.send(V.at[h, 0, xm], RRB.at[h, 0], p_xm, group=near_b)
-        yield
-        net.arrive(near_a, RLA)
-        for n in range(2):
-            U[h, n] = add(T[b + n, x], RLA[h, n], RRA[h, n])
-        z_a = net.send(U.at[h, :, zo], RZA.at[h], p_z)
         g0.wait_recv()
         V[h, 0, xp] = add(V[h, 0, xp], RFB[h, 0])
         net.send(V.at[h, 0, xp], RLB.at[h, 0], p_xp, group=near_b)
@@ -417,10 +410,17 @@
         V[h, 1, xm] = add(V[h, 1, xm], RFB[h, 1])
         net.send(V.at[h, 1, xm], RRB.at[h, 1], p_xm, group=near_b)
         yield
+        net.arrive(near_a, RLA)
+        for n in range(2):
+            U[h, n] = add(T[b + n, x], RLA[h, n], RRA[h, n])
+        z_a = net.send(U.at[h, :, zo], RZA.at[h], p_z)
+        over[3].wait_recv()
+        V[h, :, x] = add(T[B, x, zl], RZB[h, :, x])
+        yield
         z_a.wait_recv()
-        F[two[0]] = total_of(U[h, :, zl], RZA[h])
+        F[A] = total_of(U[h, :, zl], RZA[h])
         net.arrive(near_b, RLB)
-        F[two[1]] = total_of(V[h, :, x], RLB[h], RRB[h])
+        F[B] = total_of(V[h, :, x], RLB[h], RRB[h])
         yield
 
     def values():
@@ -469,19 +469,19 @@
     next(peaks0)
     next(reduce0)
     next(gather1)
-    score(4, 4)
+    score(4, 2)
+    next(reduce0)
+    score(6, 2)
     next(peaks1)
-    next(reduce0)
     value(4, 1)
     next(peaks1)
     value(5, 1)
+    next(reduce0)
+    value(6, 1)
     next(peaks1)
-    value(6, 1)
+    value(7, 1)
     next(reduce0)
-    value(7, 1)
     next(peaks1)
-    next(reduce1)
-    next(sum_up)
     next(reduce1)
     next(sum_up)
     next(reduce0)
@@ -490,6 +490,9 @@
     next(reduce0)
     next(reduce1)
     next(sum_up)
+    next(reduce1)
+    next(sum_up)
+    next(reduce1)
     next(weights)
     next(reduce1)
 

time: 103 us -> 98.8 us (0.959); the launches traced: 102 us -> 98.6 us
  Pallas kernels: 100 us -> 97.2 us
    pallas_call x1, Pallas kernels: 100 us -> 97.2 us  [per_device(): pl.pallas_call(kernel, out_shape=jax.ShapeDtypeStruct((32, 8 * VDIM), bf)...]
where the time goes in v6:
time: 98.8 us; the launch traced here: 98.6 us
  Pallas kernels  97.2 us (98%)
  local copies, waits for them, and re-layouts  1.47 us (1%)
    pallas_call x1, Pallas kernels, per_device(): pl.pallas_call(kernel, out_shape=jax.ShapeDtypeStruct((32, 8 * VDIM), bf)...  97.2 us

profile of v6, /device:TPU:0, one launch (start us, length us, event | category | flops | bytes accessed | tf_op | source)
XLA Modules:
  0.0 98.6 jit_solution(14730438840012916959)
XLA Ops:
  0.0 97.2 %shard_map.73 = bf16[32,1024]{1,0:T(8,128)(2,1)} custom-call(s32[8]{0:T(128)} %len_ref.1, f32[1,128]{1,0:T(1,128)} %constant.5.freq_ref, bf16[32,1536]{1,0:T(8,128)(2,1)} %bitcast.6, bf16[12,24576]{1,0:T(8,128)(2,1)} %q_ref.1, bf16[4,32768]{1,0:T(4,128)(2,1)} %kv_ref.1, bf16[8,576,512]{2,1,0:T(8,128)(2,1)} %bitcast.4, bf16[32,576]{1,0:T(8,128)(2,1)} %bitcast.7), custom_call_target="tpu_custom_call" | custom-call | tf_op jit(solution)/shard_map/pallas_call | solution.py:517
  97.2 1.5 %copy.9 = bf16[4,8,1024]{2,1,0:T(8,128)(2,1)} copy(bf16[4,8,1024]{2,1,0:T(8,128)(2,1)} %bitcast.5) | data formatting | bytes 131072

commit v7 on v6

--- a/solution.py
+++ b/solution.py
@@ -19,7 +19,7 @@
 WIDE = KVL + 128
 LOG2E = 1.4426950408889634
 POOL = 40
-GROUPS = 73
+GROUPS = 70
 
 
 class Copies:
@@ -58,7 +58,7 @@
 def kernel(
     len_ref, freq_ref, ql_ref, q_ref, kv_ref, cache_ref, new_ref, out_ref,
     QIN, KVIN, NEW, MOVE, SN, X, LAND, QLS, W, KC, E, QR, WV,
-    G, K, O, NB, RD, T, V, U, RFA, RLA, RRA, RZA, RFB, RLB, RRB, RZB, S, M, L, sums, ml_send, ml_recv, SC, SCT, F,
+    G, K, KR, O, NB, RD, T, V, U, RFA, RLA, RRA, RZA, RFB, RLB, RRB, RZB, S, M, L, sums, ml_send, ml_recv, SC, SCT, F,
     send_sem, recv_sem, load_sem, all_send, all_recv,
 ):
     di, gi = lax.axis_index("dp"), lax.axis_index("grp")
@@ -150,6 +150,10 @@
     MOVE[1] = (was == half).astype(f32).astype(bf)
     MOVE[2] = (was == ((to // 4) % 8) * 16 + (to % 4) * 4 + to // 32).astype(f32).astype(bf)
     MOVE[3] = (was == (to % 8) * 32 + to // 8).astype(f32).astype(bf)
+    loads[4].wait()
+    for r in range(8):
+        KR[r, ROPE * (r % 2) : ROPE * (r % 2) + ROPE] = K[r, KVL:WIDTH]
+        KR[r, ROPE * (1 - r % 2) : ROPE * (1 - r % 2) + ROPE] = jnp.zeros((ROPE, 512), bf)
     SC[...] = jnp.zeros_like(SC)
     ml_send[...] = jnp.zeros_like(ml_send)
 
@@ -209,27 +213,31 @@
         move = MOVE[2, 0:128, 0:128]
         absorbed = jnp.dot(move, QR[h, :, :, 0:KVL].reshape(128, KVL), preferred_element_type=f32)
         rotary = jnp.dot(move, rotary.reshape(128, 128).astype(bf), preferred_element_type=f32)
-        G[span, pl.ds(gi, 1), :, 0:KVL] = absorbed.astype(bf).reshape(4, 1, 32, KVL)
-        G[span, pl.ds(gi, 1), :, KVL:WIDTH] = rotary[:, :ROPE].astype(bf).reshape(4, 1, 32, ROPE)
-
-    def new_scores(h):
+        for n in range(2):
+            one, two = slice(64 * n, 64 * n + 32), slice(64 * n + 32, 64 * n + 64)
+            G[2 * h + n, gi, :, 0:KVL] = absorbed[one].astype(bf)
+            G[2 * h + n, gi, :, KVL : 2 * KVL] = absorbed[two].astype(bf)
+            both = jnp.where(lane[0:32] < ROPE, rotary[one], pltpu.roll(rotary[two], ROPE, 1))
+            G[2 * h + n, gi, :, 2 * KVL :] = both.astype(bf)
+        return absorbed.astype(bf), rotary.astype(bf)
+
+    def new_scores(h, absorbed, rotary):
         query = lax.broadcasted_iota(jnp.int32, (128, 32), 0)
         key = lax.broadcasted_iota(jnp.int32, (128, 32), 1)
         live = (key % 8 == 4 * h + query // 32) & (key // 8 <= query % 4)
-        score = lax.dot_general(
-            G[pl.ds(4 * h, 4), pl.ds(gi, 1)].reshape(128, WIDTH), NEW[...], nt,
-            preferred_element_type=f32,
+        score = lax.dot_general(absorbed, NEW[:, 0:KVL], nt, preferred_element_type=f32)
+        score = score + lax.dot_general(
+            rotary[:, 0:ROPE], NEW[:, KVL:WIDTH], nt, preferred_element_type=f32
         )
         SN[pl.ds(128 * h, 128)] = jnp.where(live, score * to_log2, -1e30)
 
     def gather(h):
-        b = 4 * h
-        A, B = (b, 2), (b + 2, 2)
+        A, B, every, upper, lower = 2 * h, 2 * h + 1, slice(0, 32), slice(0, 16), slice(16, 32)
         s_l, s_r, s_z = p_xm, p_xp, p_z
         s_lz, s_rz, s_f, s_fz = at(xm, zo, c), at(xp, zo, c), p_x2, at(x2, zo, c)
 
-        def go(span, slot, peer, group=None):
-            block = G.at[pl.ds(span[0], span[1]), slot]
+        def go(pair, slot, peer, group=None, part=every):
+            block = G.at[pair, slot, part]
             return net.send(block, block, peer, group=group)
 
         mate, far, far_a, far_b = net.group(), net.group(), net.group(), net.group()
@@ -240,37 +248,37 @@
         z_a = go(A, gi, p_z)
         l_b, r_b = go(B, gi, p_xp), go(B, gi, p_xm)
         l_a, r_a = go(A, gi, p_xp), go(A, gi, p_xm)
-        share((b, 4), gi)
+        share(pl.ds(2 * h, 2), gi)
         z_b = go(B, gi, p_z)
         yield
         z_a.wait_recv()
         lz_a, rz_a = go(A, s_z, p_xp), go(A, s_z, p_xm)
         share(A, s_z)
         l_b.wait_recv()
-        f0_b, lz_b = go((b + 2, 1), s_l, p_xp), go(B, s_l, p_z)
+        f0_b, lz_b = go(B, s_l, p_xp, part=upper), go(B, s_l, p_z)
         share(B, s_l)
         r_b.wait_recv()
-        f1_b, rz_b = go((b + 3, 1), s_r, p_xm), go(B, s_r, p_z)
+        f1_b, rz_b = go(B, s_r, p_xm, part=lower), go(B, s_r, p_z)
         share(B, s_r)
         l_a.wait_recv()
-        go((b, 1), s_l, p_xp, far)
+        go(A, s_l, p_xp, far, upper)
         share(A, s_l)
         r_a.wait_recv()
-        go((b + 1, 1), s_r, p_xm, far)
+        go(A, s_r, p_xm, far, lower)
         share(A, s_r)
         yield
         lz_a.wait_recv()
-        go((b, 1), s_lz, p_xp, far_a)
+        go(A, s_lz, p_xp, far_a, upper)
         share(A, s_lz)
         rz_a.wait_recv()
-        go((b + 1, 1), s_rz, p_xm, far_a)
+        go(A, s_rz, p_xm, far_a, lower)
         share(A, s_rz)
         f0_b.wait_recv()
-        go((b + 2, 1), s_f, p_z, far_b)
+        go(B, s_f, p_z, far_b, upper)
         f1_b.wait_recv()
-        go((b + 3, 1), s_f, p_z, far_b)
+        go(B, s_f, p_z, far_b, lower)
         share(B, s_f)
-        net.arrive(far, G.at[pl.ds(b, 2), 0])
+        net.arrive(far, G.at[0, 0])
         share(A, s_f)
         yield
         z_b.wait_recv()
@@ -279,28 +287,33 @@
         share(B, s_lz)
         rz_b.wait_recv()
         share(B, s_rz)
-        net.arrive(far_a, G.at[pl.ds(b, 2), 0])
+        net.arrive(far_a, G.at[0, 0])
         share(A, s_fz)
-        net.arrive(far_b, G.at[pl.ds(b, 2), 0])
+        net.arrive(far_b, G.at[0, 0])
         share(B, s_fz)
         yield
-        net.arrive(mate, G.at[pl.ds(b, 4), 0:8])
+        net.arrive(mate, G.at[pl.ds(2 * h, 2), 0:8])
         yield
 
     lanes = lax.broadcasted_iota(jnp.int32, (512, 128), 1)
     key_at = lax.broadcasted_iota(jnp.int32, (1, 512), 1) + gi * 512
     own_rows = pl.ds(gi * 32, 32)
 
-    def score_one(r, carry):
-        s = jnp.dot(G[r].reshape(512, WIDTH), K[r], preferred_element_type=f32) * to_log2
-        s = jnp.where(key_at < len_ref[r], s, -1e30)
-        S[r % 4] = s
-        peak = jnp.maximum(jnp.max(s, 1, keepdims=True), -1e29)
-        M[r] = jnp.broadcast_to(peak, (512, 128))
-        M[r, own_rows, :] = jnp.maximum(
-            M[r, own_rows, :], jnp.max(SN[pl.ds(r * 32, 32), :], 1, keepdims=True)
-        )
-        ml_send[r // 4, 0, pl.ds(r % 4, 1), :] = jnp.transpose(M[r])[0:1]
+    def score_pair(pair, carry):
+        turned = G[pair, :, :, 2 * KVL :].reshape(512, 2 * ROPE)
+        for n in range(2):
+            r = 2 * pair + n
+            plain = G[pair, :, :, KVL * n : KVL * (n + 1)].reshape(512, KVL)
+            s = jnp.dot(plain, K[r, 0:KVL], preferred_element_type=f32)
+            s = (s + jnp.dot(turned, KR[r], preferred_element_type=f32)) * to_log2
+            s = jnp.where(key_at < len_ref[r], s, -1e30)
+            S[r % 4] = s
+            peak = jnp.maximum(jnp.max(s, 1, keepdims=True), -1e29)
+            M[r] = jnp.broadcast_to(peak, (512, 128))
+            M[r, own_rows, :] = jnp.maximum(
+                M[r, own_rows, :], jnp.max(SN[pl.ds(r * 32, 32), :], 1, keepdims=True)
+            )
+            ml_send[r // 4, 0, pl.ds(r % 4, 1), :] = jnp.transpose(M[r])[0:1]
         return carry
 
     def value_one(r, carry):
@@ -316,31 +329,30 @@
         return carry
 
     def score(first, count):
-        lax.fori_loop(first, first + count, score_one, 0)
+        lax.fori_loop(first // 2, (first + count) // 2, score_pair, 0)
 
     def value(first, count):
         lax.fori_loop(first, first + count, value_one, 0)
 
     def butterfly(n, join):
-        total = ml_send[n, 0]
-        for stage, peer in ((0, p_c), (1, p_z)):
-            copy = net.send(ml_send.at[n, stage], ml_recv.at[n, stage], peer)
-            yield
-            copy.wait_recv()
-            total = join(total, ml_recv[n, stage])
-            ml_send[n, stage + 1] = total
-        last = net.group()
-        for j, p in enumerate((p_xp, p_xm, p_x2)):
-            net.send(ml_send.at[n, 2], ml_recv.at[n, 2 + j], p, group=last)
-        yield
-        net.arrive(last, ml_recv.at[n, 2:5])
-        for j in range(3):
-            total = join(total, ml_recv[n, 2 + j])
-        ml_send[n, 3] = total
+        copy = net.send(ml_send.at[n, 0], ml_recv.at[n, 0], p_c)
+        yield
+        copy.wait_recv()
+        total = join(ml_send[n, 0], ml_recv[n, 0])
+        ml_send[n, 1] = total
+        others = net.group()
+        for j in range(1, 8):
+            peer = (gi + 2 * j) % 16
+            net.send(ml_send.at[n, 1], ml_recv.at[n, j], peer, group=others)
+        yield
+        net.arrive(others, ml_recv.at[n, 1:8])
+        for j in range(1, 8):
+            total = join(total, ml_recv[n, j])
+        ml_send[n, 2] = total
 
     def peaks(h):
         yield from butterfly(h, jnp.maximum)
-        factor = jnp.exp2(ml_send[h, 0] - ml_send[h, 3])
+        factor = jnp.exp2(ml_send[h, 0] - ml_send[h, 2])
         sums[4 * h : 4 * h + 4] = sums[4 * h : 4 * h + 4] * factor[0:4]
         SC[0:8] = factor
         SCT[h] = jnp.transpose(SC[...])
@@ -349,7 +361,7 @@
     def totals():
         ml_send[2, 0] = sums[...]
         yield from butterfly(2, jnp.add)
-        SC[0:8] = ml_send[2, 3]
+        SC[0:8] = ml_send[2, 2]
         SCT[2] = jnp.transpose(SC[...])
         yield
 
@@ -443,18 +455,17 @@
     peaks0, peaks1 = peaks(0), peaks(1)
     reduce0, reduce1 = reduce(0), reduce(1)
     weights, sum_up = values(), totals()
-    place(0)
+    queries0 = place(0)
     next(gather0)
-    place(1)
-    new_scores(0)
-    new_scores(1)
+    queries1 = place(1)
+    new_scores(0, *queries0)
+    new_scores(1, *queries1)
     next(weights)
     next(gather0)
     next(gather0)
     next(gather1)
     next(weights)
     next(gather0)
-    loads[4].wait()
     next(gather0)
     score(0, 4)
     next(peaks0)
@@ -463,35 +474,29 @@
     next(peaks0)
     value(2, 2)
     next(gather1)
-    next(peaks0)
     next(weights)
-    next(gather1)
     next(peaks0)
     next(reduce0)
     next(gather1)
-    score(4, 2)
     next(reduce0)
-    score(6, 2)
+    next(gather1)
+    score(4, 4)
     next(peaks1)
-    value(4, 1)
+    value(4, 2)
     next(peaks1)
-    value(5, 1)
     next(reduce0)
-    value(6, 1)
-    next(peaks1)
-    value(7, 1)
+    value(6, 2)
     next(reduce0)
     next(peaks1)
     next(reduce1)
     next(sum_up)
     next(reduce0)
+    next(sum_up)
     next(reduce1)
-    next(sum_up)
     next(reduce0)
     next(reduce1)
     next(sum_up)
     next(reduce1)
-    next(sum_up)
     next(reduce1)
     next(weights)
     next(reduce1)
@@ -533,8 +538,9 @@
             pltpu.VMEM((8, 32, WIDE), bf),
             pltpu.VMEM((2, 8, 16, WIDE), bf),
             pltpu.VMEM((8, KVL, VDIM), bf),
-            pltpu.VMEM((8, 16, 32, WIDTH), bf),
+            pltpu.VMEM((4, 16, 32, 2 * WIDTH), bf),
             pltpu.VMEM((8, WIDTH, 512), bf),
+            pltpu.VMEM((8, 2 * ROPE, 512), bf),
             pltpu.VMEM((8, 512, KVL), f32),
             pltpu.VMEM((8, 4, 2, 2, 32, KVL), bf),
             pltpu.VMEM((8, 4, 2, 32, KVL), bf),
@@ -553,8 +559,8 @@
             pltpu.VMEM((8, 512, 128), f32),
             pltpu.VMEM((512, 128), f32),
             pltpu.VMEM((8, 512), f32),
-            pltpu.VMEM((3, 4, 8, 512), f32),
-            pltpu.VMEM((3, 5, 8, 512), f32),
+            pltpu.VMEM((3, 3, 8, 512), f32),
+            pltpu.VMEM((3, 8, 8, 512), f32),
             pltpu.VMEM((128, 512), f32),
             pltpu.VMEM((3, 512, 128), f32),
             pltpu.VMEM((8, 32, KVL), f32),

time: 98.8 us -> 92.3 us (0.934)
  Pallas kernels: 97.2 us -> 90.6 us
    pallas_call x1, Pallas kernels: 97.2 us -> 90.6 us  [per_device(): pl.pallas_call(kernel, out_shape=jax.ShapeDtypeStruct((32, 8 * VDIM), bf)...]
where the time goes in v7:
time: 92.3 us; the launch traced here: 92.1 us
  Pallas kernels  90.6 us (98%)
  local copies, waits for them, and re-layouts  1.47 us (2%)
    pallas_call x1, Pallas kernels, per_device(): pl.pallas_call(kernel, out_shape=jax.ShapeDtypeStruct((32, 8 * VDIM), bf)...  90.6 us

profile of v7, /device:TPU:0, one launch (start us, length us, event | category | flops | bytes accessed | tf_op | source)
XLA Modules:
  0.0 92.1 jit_solution(6127741998700119507)
XLA Ops:
  0.0 90.6 %shard_map.73 = bf16[32,1024]{1,0:T(8,128)(2,1)} custom-call(s32[8]{0:T(128)} %len_ref.1, f32[1,128]{1,0:T(1,128)} %constant.5.freq_ref, bf16[32,1536]{1,0:T(8,128)(2,1)} %bitcast.6, bf16[12,24576]{1,0:T(8,128)(2,1)} %q_ref.1, bf16[4,32768]{1,0:T(4,128)(2,1)} %kv_ref.1, bf16[8,576,512]{2,1,0:T(8,128)(2,1)} %bitcast.4, bf16[32,576]{1,0:T(8,128)(2,1)} %bitcast.7), custom_call_target="tpu_custom_call" | custom-call | tf_op jit(solution)/shard_map/pallas_call | solution.py:522
  90.6 1.5 %copy.9 = bf16[4,8,1024]{2,1,0:T(8,128)(2,1)} copy(bf16[4,8,1024]{2,1,0:T(8,128)(2,1)} %bitcast.5) | data formatting | bytes 131072

commit v8 on v7

--- a/solution.py
+++ b/solution.py
@@ -87,14 +87,22 @@
         d = (me + 37 * j) % 128
         return d // 16, d % 16
 
-    def greet(j, carry):
+    def six(one):
+        def body(n, carry):
+            for j in range(6):
+                one(6 * n + j + 1)
+            return carry
+
+        lax.fori_loop(0, 21, body, 0)
+        one(127)
+
+    def greet(j):
         dd, gg = there(j)
         pl.semaphore_signal(
             barrier, inc=1, device_id={"dp": dd, "grp": gg}, device_id_type=MESH
         )
-        return carry
-
-    lax.fori_loop(1, 128, greet, 0)
+
+    six(greet)
     bf, f32 = jnp.bfloat16, jnp.float32
     nt = (((1,), (1,)), ((), ()))
 
@@ -124,7 +132,7 @@
     for j in range(1, 8):
         net.send(QLS.at[0, rows], QLS.at[8 - j, rows], (di + j) % 8, "dp", first)
 
-    def deal(j, carry):
+    def deal(j):
         dd, gg = there(j)
         pltpu.make_async_remote_copy(
             src_ref=X.at[8 * gg + dd],
@@ -134,9 +142,8 @@
             device_id={"dp": dd, "grp": gg},
             device_id_type=MESH,
         ).start()
-        return carry
-
-    lax.fori_loop(1, 128, deal, 0)
+
+    six(deal)
 
     to = lax.broadcasted_iota(jnp.int32, (256, 256), 0)
     was = lax.broadcasted_iota(jnp.int32, (256, 256), 1)

time: 92.3 us -> 91.4 us (level)
  no operation moved by 1% of the time
where the time goes in v8:
time: 91.4 us; the launch traced here: 91.2 us
  Pallas kernels  89.7 us (98%)
  local copies, waits for them, and re-layouts  1.47 us (2%)
    pallas_call x1, Pallas kernels, per_device(): pl.pallas_call(kernel, out_shape=jax.ShapeDtypeStruct((32, 8 * VDIM), bf)...  89.7 us

profile of v8, /device:TPU:0, one launch (start us, length us, event | category | flops | bytes accessed | tf_op | source)
XLA Modules:
  0.0 91.2 jit_solution(16353350577080550752)
XLA Ops:
  0.0 89.7 %shard_map.73 = bf16[32,1024]{1,0:T(8,128)(2,1)} custom-call(s32[8]{0:T(128)} %len_ref.1, f32[1,128]{1,0:T(1,128)} %constant.5.freq_ref, bf16[32,1536]{1,0:T(8,128)(2,1)} %bitcast.6, bf16[12,24576]{1,0:T(8,128)(2,1)} %q_ref.1, bf16[4,32768]{1,0:T(4,128)(2,1)} %kv_ref.1, bf16[8,576,512]{2,1,0:T(8,128)(2,1)} %bitcast.4, bf16[32,576]{1,0:T(8,128)(2,1)} %bitcast.7), custom_call_target="tpu_custom_call" | custom-call | tf_op jit(solution)/shard_map/pallas_call | solution.py:529
  89.8 1.5 %copy.9 = bf16[4,8,1024]{2,1,0:T(8,128)(2,1)} copy(bf16[4,8,1024]{2,1,0:T(8,128)(2,1)} %bitcast.5) | data formatting | bytes 131072

commit v9 on v8

--- a/solution.py
+++ b/solution.py
@@ -19,7 +19,8 @@
 WIDE = KVL + 128
 LOG2E = 1.4426950408889634
 POOL = 40
-GROUPS = 70
+FAR_FIRST = (2, 6, 1, 3, 5, 7, 4)
+GROUPS = 72
 
 
 class Copies:
@@ -129,7 +130,7 @@
     net = Copies(send_sem, recv_sem)
     rows = pl.ds(pl.multiple_of(c * 16, 16), 16)
     first = net.group()
-    for j in range(1, 8):
+    for j in FAR_FIRST:
         net.send(QLS.at[0, rows], QLS.at[8 - j, rows], (di + j) % 8, "dp", first)
 
     def deal(j):
@@ -203,7 +204,7 @@
     for h in range(2):
         span = pl.ds(16 * h, 16)
         heads.append(net.group())
-        for j in range(1, 8):
+        for j in FAR_FIRST:
             net.send(E.at[j, span], QR.at[h, di], (di + j) % 8, "dp", heads[h])
         QR[h, di] = E[0, span]
     loads[3].wait()
@@ -247,15 +248,18 @@
             block = G.at[pair, slot, part]
             return net.send(block, block, peer, group=group)
 
-        mate, far, far_a, far_b = net.group(), net.group(), net.group(), net.group()
+        mate, far, far_a, far_b = {}, net.group(), net.group(), net.group()
+        for pair in (A, B):
+            mate[pair] = net.group()
 
         def share(span, slot):
-            go(span, slot, p_c, mate)
+            go(span, slot, p_c, mate[span])
 
         z_a = go(A, gi, p_z)
         l_b, r_b = go(B, gi, p_xp), go(B, gi, p_xm)
         l_a, r_a = go(A, gi, p_xp), go(A, gi, p_xm)
-        share(pl.ds(2 * h, 2), gi)
+        share(A, gi)
+        share(B, gi)
         z_b = go(B, gi, p_z)
         yield
         z_a.wait_recv()
@@ -288,18 +292,21 @@
         net.arrive(far, G.at[0, 0])
         share(A, s_f)
         yield
+        net.arrive(far_a, G.at[0, 0])
+        share(A, s_fz)
         z_b.wait_recv()
         share(B, s_z)
+        yield
+        net.arrive(mate[A], G.at[A, 0:8])
+        yield
         lz_b.wait_recv()
         share(B, s_lz)
         rz_b.wait_recv()
         share(B, s_rz)
-        net.arrive(far_a, G.at[0, 0])
-        share(A, s_fz)
         net.arrive(far_b, G.at[0, 0])
         share(B, s_fz)
         yield
-        net.arrive(mate, G.at[pl.ds(2 * h, 2), 0:8])
+        net.arrive(mate[B], G.at[B, 0:8])
         yield
 
     lanes = lax.broadcasted_iota(jnp.int32, (512, 128), 1)
@@ -379,6 +386,8 @@
         return total
 
     def add(*terms):
+        if len(terms) == 2:
+            return terms[0] + terms[1]
         return total_of(*terms).astype(bf)
 
     def reduce(h):
@@ -474,7 +483,10 @@
     next(weights)
     next(gather0)
     next(gather0)
-    score(0, 4)
+    next(gather0)
+    score(0, 2)
+    next(gather0)
+    score(2, 2)
     next(peaks0)
     next(gather1)
     value(0, 2)
@@ -487,7 +499,10 @@
     next(gather1)
     next(reduce0)
     next(gather1)
-    score(4, 4)
+    next(gather1)
+    score(4, 2)
+    next(gather1)
+    score(6, 2)
     next(peaks1)
     value(4, 2)
     next(peaks1)

time: 91.4 us -> 91.5 us (level)
  no operation moved by 1% of the time
where the time goes in v9:
time: 91.5 us; the launch traced here: 91.3 us
  Pallas kernels  89.9 us (98%)
  local copies, waits for them, and re-layouts  1.47 us (2%)
    pallas_call x1, Pallas kernels, per_device(): pl.pallas_call(kernel, out_shape=jax.ShapeDtypeStruct((32, 8 * VDIM), bf)...  89.9 us

profile of v9, /device:TPU:0, one launch (start us, length us, event | category | flops | bytes accessed | tf_op | source)
XLA Modules:
  0.0 91.3 jit_solution(7279018441282999988)
XLA Ops:
  0.0 89.9 %shard_map.73 = bf16[32,1024]{1,0:T(8,128)(2,1)} custom-call(s32[8]{0:T(128)} %len_ref.1, f32[1,128]{1,0:T(1,128)} %constant.5.freq_ref, bf16[32,1536]{1,0:T(8,128)(2,1)} %bitcast.6, bf16[12,24576]{1,0:T(8,128)(2,1)} %q_ref.1, bf16[4,32768]{1,0:T(4,128)(2,1)} %kv_ref.1, bf16[8,576,512]{2,1,0:T(8,128)(2,1)} %bitcast.4, bf16[32,576]{1,0:T(8,128)(2,1)} %bitcast.7), custom_call_target="tpu_custom_call" | custom-call | tf_op jit(solution)/shard_map/pallas_call | solution.py:544
  89.9 1.5 %copy.9 = bf16[4,8,1024]{2,1,0:T(8,128)(2,1)} copy(bf16[4,8,1024]{2,1,0:T(8,128)(2,1)} %bitcast.5) | data formatting | bytes 131072
